TPU v7x, 32 devices: a whole 2x2x4 slice. The times are simulated.
32 devices in a mesh: dp: 8 (over y, x, core), seq: 4 (over z).
Axes of the slice: x: 2, y: 2, z: 4, core: 2. Of those that a mesh axis runs over, the one named last changes fastest.
Arguments:
- tokens: float32 [8, 1024, 1024], P('dp', 'seq'), may hold values from -6 to 6
- ln_params: float32 [4, 1024], P(None, ('dp', 'seq')), may hold values from 0.25 to 1.75
- qkv_weight: float32 [1024, 3, 1024], P(('dp', 'seq')), may hold values from -0.1875 to 0.1875
- out_weight: float32 [1024, 1024], P(('dp', 'seq')), may hold values from -3 to 3
- ffn_weight: float32 [4096, 3, 1024], P(('dp', 'seq')), may hold values from -0.1875 to 0.1875
- lengths: int32 [8, 16], P('dp'), may hold values from 1 to 896, 1024 in all within a row
- cotangent: float32 [8, 1024, 1024], P('dp', 'seq'), may hold values from -6 to 6
Outputs:
- output: float32 [8, 1024, 1024], P('dp', 'seq')
- input_grad: float32 [8, 1024, 1024], P('dp', 'seq')
- ln_grad: float32 [4, 1024], P(None, ('dp', 'seq'))
- qkv_grad: float32 [1024, 3, 1024], P(('dp', 'seq'))
- out_weight_grad: float32 [1024, 1024], P(('dp', 'seq'))
- ffn_grad: float32 [4096, 3, 1024], P(('dp', 'seq'))
Inputs may be any that keep to these rules, and one draw needn't show every extreme that they name: Each row's 16 lengths sum to 1024; one of them is exactly 896.
All inputs are finite; a program needn't handle non-finite values.
Results may differ from a plain program's by a relative error of at most 0.013.
The roundings to bfloat16 on the way count: a program that leaves them out, or rounds other values in their place, can miss the bound.
Values may be sent and summed in bfloat16 or wider, within the bound.
A program may use at most 320 MiB of HBM per device.

v0:
```python
import math

import jax
import jax.numpy as jnp
from jax import lax
from jax.sharding import PartitionSpec as P

HEAD_DIM = 64


def segment_layout(seg_lengths, first, count):
    ends = jnp.cumsum(seg_lengths)
    place = first + jnp.arange(count, dtype=jnp.int32)
    done = place[:, None] >= ends[None, :]
    segment = jnp.sum(done.astype(jnp.int32), axis=1)
    start = jnp.sum(jnp.where(done, seg_lengths[None, :], 0), axis=1)
    return (segment, place - start)


def angles(place, half):
    rate = jnp.exp(jnp.arange(half, dtype=jnp.float32) * (-math.log(10000.0) / half))
    angle = place.astype(jnp.float32)[:, None] * rate[None, :]
    return (jnp.cos(angle)[:, None, :], jnp.sin(angle)[:, None, :])


def rotate(value, cosine, sine):
    half = value.shape[-1] // 2
    first = value[..., :half]
    second = value[..., half:]
    return jnp.concatenate(
        [first * cosine - second * sine, second * cosine + first * sine], axis=-1
    )


def rotate_back(grad, cosine, sine):
    half = grad.shape[-1] // 2
    first = grad[..., :half]
    second = grad[..., half:]
    return jnp.concatenate(
        [first * cosine + second * sine, second * cosine - first * sine], axis=-1
    )


def layer_norm(value, gain, shift):
    mean = jnp.mean(value, axis=-1, keepdims=True)
    centred = value - mean
    var = jnp.mean(centred * centred, axis=-1, keepdims=True)
    scale = lax.rsqrt(var + 1e-05)
    normal = centred * scale
    return (normal * gain + shift, normal, scale)


def norm_back(grad, normal, scale, gain):
    scaled = grad * gain
    return scale * (
        scaled
        - jnp.mean(scaled, axis=-1, keepdims=True)
        - normal * jnp.mean(scaled * normal, axis=-1, keepdims=True)
    )


def make_forward(rows_in, piece):
    gate = jnp.einsum("td,kd->tk", rows_in, piece[:, 0], preferred_element_type=jnp.float32)
    up_proj = jnp.einsum("td,kd->tk", rows_in, piece[:, 1], preferred_element_type=jnp.float32)
    hidden = (jax.nn.silu(gate) * up_proj).astype(jnp.bfloat16)
    return jnp.einsum("tk,kd->td", hidden, piece[:, 2], preferred_element_type=jnp.float32)


def make_backward(rows_in, grad_in, piece):
    gate = jnp.einsum("td,kd->tk", rows_in, piece[:, 0], preferred_element_type=jnp.float32)
    up_proj = jnp.einsum("td,kd->tk", rows_in, piece[:, 1], preferred_element_type=jnp.float32)
    sigma = jax.nn.sigmoid(gate)
    active = jax.nn.silu(gate)
    hidden = (active * up_proj).astype(jnp.bfloat16)
    d_hidden = jnp.einsum("td,kd->tk", grad_in, piece[:, 2], preferred_element_type=jnp.float32)
    d_gate = (d_hidden * up_proj * (sigma * (1.0 + gate * (1.0 - sigma)))).astype(jnp.bfloat16)
    d_up = (d_hidden * active).astype(jnp.bfloat16)
    d_norm = jnp.einsum("tk,kd->td", d_gate, piece[:, 0], preferred_element_type=jnp.float32)
    d_norm = d_norm + jnp.einsum("tk,kd->td", d_up, piece[:, 1], preferred_element_type=jnp.float32)
    return (d_norm, hidden, d_gate, d_up)


def make_terms(kept_hidden, kept_gate, kept_up, rows_in, grad_in):
    gate_term = jnp.einsum("tk,td->kd", kept_gate, rows_in, preferred_element_type=jnp.float32)
    up_term = jnp.einsum("tk,td->kd", kept_up, rows_in, preferred_element_type=jnp.float32)
    down_term = jnp.einsum("tk,td->kd", kept_hidden, grad_in, preferred_element_type=jnp.float32)
    return jnp.stack([gate_term, up_term, down_term], axis=1)


def body(tokens, ln_params, qkv_weight, out_weight, ffn_weight, lengths, cotangent):
    count = tokens.shape[1]
    width = tokens.shape[2]
    total = count * lax.axis_size("seq")
    heads = width // HEAD_DIM
    resid = tokens.reshape(count, width)
    grad_out = cotangent.reshape(count, width)
    row_lengths = lengths[0]
    key_seg, key_place = segment_layout(row_lengths, 0, total)
    query_seg, query_place = segment_layout(row_lengths, lax.axis_index("seq") * count, count)
    same = query_seg[:, None] == key_seg[None, :]
    cosine, sine = angles(query_place, HEAD_DIM // 2)
    masters = (
        ln_params.astype(jnp.bfloat16),
        qkv_weight.astype(jnp.bfloat16),
        out_weight.astype(jnp.bfloat16),
    )
    ln_all, qkv_all, out_all = (
        lax.all_gather(masters[0], ("dp", "seq"), axis=1, tiled=True),
        lax.all_gather(masters[1], ("dp", "seq"), axis=0, tiled=True),
        lax.all_gather(masters[2], ("dp", "seq"), axis=0, tiled=True),
    )
    gains = ln_all.astype(jnp.float32)
    normed1, normal1, scale1 = layer_norm(resid, gains[0], gains[1])
    normed1_low = normed1.astype(jnp.bfloat16)
    qkv = jnp.einsum("td,dkf->tkf", normed1_low, qkv_all, preferred_element_type=jnp.float32)
    query_low = rotate(qkv[:, 0].reshape(count, heads, HEAD_DIM), cosine, sine).astype(jnp.bfloat16)
    key_low = rotate(qkv[:, 1].reshape(count, heads, HEAD_DIM), cosine, sine).astype(jnp.bfloat16)
    value_low = qkv[:, 2].astype(jnp.bfloat16)
    keys_all, values_all = (
        lax.all_gather(key_low.reshape(count, width), "seq", axis=0, tiled=True),
        lax.all_gather(value_low, "seq", axis=0, tiled=True),
    )
    q_heads = query_low.transpose(1, 0, 2)
    k_heads = keys_all.reshape(total, heads, HEAD_DIM).transpose(1, 0, 2)
    v_heads = values_all.reshape(total, heads, HEAD_DIM).transpose(1, 0, 2)

    def head_scores(q_head, k_head):
        score = jnp.einsum("qd,kd->qk", q_head, k_head, preferred_element_type=jnp.float32) * 0.125
        return jnp.where(same, score, -1e30)

    def forward_head(parts):
        q_head, k_head, v_head = parts
        score = head_scores(q_head, k_head)
        top = jnp.max(score, axis=1, keepdims=True)
        weight = jnp.exp(score - top)
        tally = jnp.sum(weight, axis=1, keepdims=True)
        prob = (weight / tally).astype(jnp.bfloat16)
        mixed = jnp.dot(prob, v_head, preferred_element_type=jnp.float32)
        return (mixed, (top + jnp.log(tally))[:, 0])

    mixed, log_total = lax.map(forward_head, (q_heads, k_heads, v_heads))
    attended = mixed.transpose(1, 0, 2).reshape(count, width).astype(jnp.bfloat16)
    middle = resid + jnp.dot(attended, out_all, preferred_element_type=jnp.float32)
    normed2, normal2, scale2 = layer_norm(middle, gains[2], gains[3])
    normed2_low = normed2.astype(jnp.bfloat16)
    grad_low = grad_out.astype(jnp.bfloat16)
    ffn_low = ffn_weight.astype(jnp.bfloat16)
    branch = make_forward(normed2_low, lax.all_gather(ffn_low, ("dp", "seq"), axis=0, tiled=True))
    output = middle + branch
    d_norm2, kept_hidden, kept_gate, kept_up = make_backward(
        normed2_low, grad_low, lax.all_gather(ffn_low, ("dp", "seq"), axis=0, tiled=True)
    )
    ffn_grad = lax.psum_scatter(
        make_terms(kept_hidden, kept_gate, kept_up, normed2_low, grad_low),
        ("dp", "seq"),
        scatter_dimension=0,
        tiled=True,
    )
    ln_all, qkv_all, out_all = (
        lax.all_gather(masters[0], ("dp", "seq"), axis=1, tiled=True),
        lax.all_gather(masters[1], ("dp", "seq"), axis=0, tiled=True),
        lax.all_gather(masters[2], ("dp", "seq"), axis=0, tiled=True),
    )
    gains = ln_all.astype(jnp.float32)
    d_gain2 = jnp.sum(d_norm2 * normal2, axis=0)
    d_shift2 = jnp.sum(d_norm2, axis=0)
    d_middle = grad_out + norm_back(d_norm2, normal2, scale2, gains[2])
    d_middle_low = d_middle.astype(jnp.bfloat16)
    d_out_weight = jnp.einsum(
        "ta,td->ad", attended, d_middle_low, preferred_element_type=jnp.float32
    )
    d_attended = jnp.einsum(
        "td,ad->ta", d_middle_low, out_all, preferred_element_type=jnp.float32
    ).astype(jnp.bfloat16)
    d_heads = d_attended.reshape(count, heads, HEAD_DIM).transpose(1, 0, 2)

    def backward_head(parts):
        q_head, k_head, v_head, d_head, log_head = parts
        score = head_scores(q_head, k_head)
        prob = jnp.exp(score - log_head[:, None])
        d_prob = jnp.einsum("qd,kd->qk", d_head, v_head, preferred_element_type=jnp.float32)
        centre = jnp.sum(prob * d_prob, axis=1, keepdims=True)
        d_score = (0.125 * prob * (d_prob - centre)).astype(jnp.bfloat16)
        d_query = jnp.einsum("qk,kd->qd", d_score, k_head, preferred_element_type=jnp.float32)
        d_key = jnp.einsum("qk,qd->kd", d_score, q_head, preferred_element_type=jnp.float32)
        d_value = jnp.einsum(
            "qk,qd->kd", prob.astype(jnp.bfloat16), d_head, preferred_element_type=jnp.float32
        )
        return (d_query, d_key, d_value)

    d_query, d_key, d_value = lax.map(
        backward_head, (q_heads, k_heads, v_heads, d_heads, log_total)
    )
    key_terms = d_key.transpose(1, 0, 2).reshape(total, width)
    value_terms = d_value.transpose(1, 0, 2).reshape(total, width)
    key_grad, value_grad = (
        lax.psum_scatter(
            key_terms.astype(jnp.bfloat16), "seq", scatter_dimension=0, tiled=True
        ).astype(jnp.float32),
        lax.psum_scatter(
            value_terms.astype(jnp.bfloat16), "seq", scatter_dimension=0, tiled=True
        ).astype(jnp.float32),
    )
    dq_low = (
        rotate_back(d_query.transpose(1, 0, 2), cosine, sine)
        .reshape(count, width)
        .astype(jnp.bfloat16)
    )
    dk_low = (
        rotate_back(key_grad.reshape(count, heads, HEAD_DIM), cosine, sine)
        .reshape(count, width)
        .astype(jnp.bfloat16)
    )
    dv_low = value_grad.astype(jnp.bfloat16)
    d_qkv = jnp.stack([dq_low, dk_low, dv_low], axis=1)
    d_norm1 = jnp.einsum("tkf,dkf->td", d_qkv, qkv_all, preferred_element_type=jnp.float32)
    d_qkv_weight = jnp.einsum("td,tkf->dkf", normed1_low, d_qkv, preferred_element_type=jnp.float32)
    d_gain1 = jnp.sum(d_norm1 * normal1, axis=0)
    d_shift1 = jnp.sum(d_norm1, axis=0)
    input_grad = d_middle + norm_back(d_norm1, normal1, scale1, gains[0])
    ln_terms = jnp.stack([d_gain1, d_shift1, d_gain2, d_shift2], axis=0)
    ln_grad, qkv_grad, out_weight_grad = (
        lax.psum_scatter(ln_terms, ("dp", "seq"), scatter_dimension=1, tiled=True),
        lax.psum_scatter(d_qkv_weight, ("dp", "seq"), scatter_dimension=0, tiled=True),
        lax.psum_scatter(d_out_weight, ("dp", "seq"), scatter_dimension=0, tiled=True),
    )
    return (
        output.reshape(1, count, width),
        input_grad.reshape(1, count, width),
        ln_grad,
        qkv_grad,
        out_weight_grad,
        ffn_grad,
    )


def solution(mesh):
    in_specs = (
        P("dp", "seq", None),
        P(None, ("dp", "seq")),
        P(("dp", "seq"), None, None),
        P(("dp", "seq"), None),
        P(("dp", "seq"), None, None),
        P("dp", None),
        P("dp", "seq", None),
    )
    out_specs = (
        P("dp", "seq", None),
        P("dp", "seq", None),
        P(None, ("dp", "seq")),
        P(("dp", "seq"), None, None),
        P(("dp", "seq"), None),
        P(("dp", "seq"), None, None),
    )
    return jax.shard_map(body, mesh=mesh, in_specs=in_specs, out_specs=out_specs, check_vma=False)
```

profile of v0, /device:TPU:0, one launch (start us, length us, event | category | flops | bytes accessed | tf_op | source)
XLA Modules:
  0.0 2284.7 jit_solution(4999882045070970695)
XLA Ops:
  10.6 70.3 %all-gather.1 = bf16[32,32,4]{1,2,0:T(4,128)(2,1)S(1)} all-gather(bf16[1,32,4]{1,2,0:T(4,128)(2,1)S(1)} %convert_bitcast_fusion), channel_id=1, replica_groups=mesh['dp'=8,'seq'=4] {'dp','seq'}, dimensions={0}, use_global_device_ids=true | all-gather | bytes 8448 | tf_op jit(solution)/shard_map/all_gather | solution.py:108
  85.0 5.0 fusion.67
  93.7 2.1 slice.130
  99.2 38.3 %all-gather.10.cloned.1.call-done = bf16[1024,1024]{0,1:T(8,128)(2,1)} async-done(((bf16[256,1024]{0,1:T(8,128)(2,1)}), bf16[1024,1024]{0,1:T(8,128)(2,1)}) %all-gather.10.cloned.1.call-update) | async-done | bytes 2097168 | tf_op jit(solution)/shard_map/all_gather | solution.py:120
  137.5 4.8 copy.83
  142.3 41.0 %all-gather.16.cloned.1.call-done = bf16[1024,1,1024]{2,0,1:T(8,128)(2,1)} async-done(((bf16[256,1,1024]{2,0,1:T(8,128)(2,1)}), bf16[1024,1,1024]{2,0,1:T(8,128)(2,1)}) %all-gather.16.cloned.1.call-update) | async-done | bytes 2097168 | tf_op jit(solution)/shard_map/all_gather | solution.py:121
  183.3 2.9 copy.81
  186.1 3.2 copy.84
  189.3 50.0 %while.30 = (s32[]{:T(128)}, bf16[16,256,64]{1,2,0:T(8,128)(2,1)S(1)}, f32[16,256]{1,0:T(8,128)S(1)}, bf16[16,256,64]{2,1,0:T(8,128)(2,1)}, bf16[16,1024,64]{2,1...) while((s32[]{:T(128)}, ...), condition=%wide.region_9.10_spmd.clone.clone, body=%wide.region_6.9_spmd.clone.sunk.clone | while | flops 69467904 | bytes 3818593 | solution.py:141
  239.3 2.7 all-gather.12.cloned.1.call-done
  242.0 2.4 fusion.73
  245.0 153.8 %all-gather.14.cloned.1.call-done = bf16[4096,3,1024]{2,0,1:T(8,128)(2,1)} async-done(((bf16[128,3,1024]{2,0,1:T(8,128)(2,1)}), bf16[4096,3,1024]{2,0,1:T(8,128)(2,1)}) %all-gather.14.cloned.1.call-update) | async-done | bytes 25165840 | tf_op jit(solution)/shard_map/all_gather | solution.py:148
  398.8 5.7 fusion.47
  404.5 5.8 fusion.45
  410.4 7.4 multiply_convert_fusion.1
  417.8 7.3 fusion.44
  425.1 5.3 multiply_reduce_fusion.1
  433.6 2.1 copy.85
  435.7 132.9 %while.31 = (s32[]{:T(128)}, f32[16,256,64]{1,2,0:T(8,128)}, bf16[16,1024,64]{1,2,0:T(8,128)(2,1)}, bf16[16,1024,64]{1,2,0:T(8,128)(2,1)}, bf16[16,256,64]{2,1,0...) while((s32[]{:T(128)}, f32[16,256,64]{1,2,0:T(8,128)}, ...), condition=%wide.region_16.17_spmd.clone.clone, body=%wide.region_14.16_spmd.clone.sunk.clone | while | flops 170655488 | bytes 9452665 | solution.py:191
  440.4 1.9 fusion.141
  442.2 1.7 fusion.142
  448.7 1.9 fusion.141
  457.0 1.9 fusion.141
  465.3 1.9 fusion.141
  467.2 1.7 fusion.142
  473.6 1.9 fusion.141
  475.5 1.7 fusion.142
  481.9 1.9 fusion.141
  483.8 1.7 fusion.142
  490.2 1.9 fusion.141
  492.1 1.7 fusion.142
  498.5 1.9 fusion.141
  500.4 1.7 fusion.142
  506.8 1.9 fusion.141
  508.7 1.7 fusion.142
  515.1 1.9 fusion.141
  517.0 1.7 fusion.142
  523.5 1.9 fusion.141
  531.7 1.9 fusion.141
  540.0 1.9 fusion.141
  548.3 1.9 fusion.141
  550.2 1.7 fusion.142
  556.6 1.9 fusion.141
  564.9 1.9 fusion.141
  566.8 1.7 fusion.142
  568.6 3.9 copy.90
  572.7 38.2 %reduce-scatter.9.cloned.1.call-done = bf16[256,1024]{0,1:T(8,128)(2,1)} async-done(((bf16[1024,1024]{0,1:T(8,128)(2,1)}), bf16[256,1024]{0,1:T(8,128)(2,1)}) %reduce-scatter.9.cloned.1.call-update) | async-done | bytes 524304 | tf_op jit(solution)/shard_map/reduce_scatter | solution.py:197
  612.0 2.2 add_convert_fusion.3
  615.0 2.0 copy.91
  617.1 1.8 pad_maximum_fusion.6
  618.8 2.1 copy.92
  620.9 35.5 %reduce-scatter.11.cloned.1.call-done = bf16[256,1024]{1,0:T(8,128)(2,1)} async-done(((bf16[1024,1024]{1,0:T(8,128)(2,1)}), bf16[256,1024]{1,0:T(8,128)(2,1)}) %reduce-scatter.11.cloned.1.call-update) | async-done | bytes 524304 | tf_op jit(solution)/shard_map/reduce_scatter | solution.py:200
  656.4 6.3 multiply_reduce_fusion.2
  663.9 3.7 fusion.59
  667.7 7.8 fusion.55
  675.8 9.9 convolution_bitcast_fusion.5
  685.7 8.2 convolution_bitcast_fusion.6
  693.9 8.2 convolution_bitcast_fusion.4
  702.1 34.0 %pad_maximum_fusion = f32[4096,3,1024]{2,0,1:T(8,128)} fusion(f32[4096,1,1024]{2,0,1:T(8,128)} %convolution_bitcast_fusion.4, f32[4096,1,1024]{2,0,1:T(8,128)} %convolution_bitcast_fusion.5, f32[4096,1,1024]{2,0,1:T(8,128)} %convolution_bitcast_fusion.6), kind=kLoop, calls=%fused_computation.54 | loop fusion | flops 25165824 | bytes 100663296 | tf_op jit(solution)/shard_map/stack | solution.py:87
  736.2 7.4 fusion.52
  744.9 52.7 %reduce-scatter.19.cloned.1.call-done = f32[32,4]{1,0:T(8,128)} async-done(((f32[1024,4]{1,0:T(8,128)}), f32[32,4]{1,0:T(8,128)}) %reduce-scatter.19.cloned.1.call-update) | async-done | bytes 528
  799.0 145.6 %reduce-scatter.15.cloned.1.call-done = f32[32,1024]{1,0:T(8,128)} async-done(((f32[1024,1024]{1,0:T(8,128)}), f32[32,1024]{1,0:T(8,128)}) %reduce-scatter.15.cloned.1.call-update) | async-done | bytes 131088 | tf_op jit(solution)/shard_map/reduce_scatter | solution.py:225
  944.6 273.9 %reduce-scatter.13.cloned.1.call-done = f32[32,3,1024]{2,0,1:T(8,128)} async-done(((f32[1024,3,1024]{2,0,1:T(8,128)}), f32[32,3,1024]{2,0,1:T(8,128)}) %reduce-scatter.13.cloned.1.call-update) | async-done | bytes 393232 | tf_op jit(solution)/shard_map/reduce_scatter | solution.py:224
  1218.5 1059.7 %reduce-scatter.17.cloned.1.call-done = f32[128,3,1024]{2,0,1:T(8,128)} async-done(((f32[4096,3,1024]{2,0,1:T(8,128)}), f32[128,3,1024]{2,0,1:T(8,128)}) %reduce-scatter.17.cloned.1.call-update) | async-done | bytes 1572880 | tf_op jit(solution)/shard_map/reduce_scatter | solution.py:153
  (266 shorter events, 159.0 us)
Async XLA Ops:
  7.2 77.8 %all-gather.8.cloned.1.call-start = ((), (), s32[]{:S(2)}) async-start(), calls=%async_computation.6 | async-start | bytes 6488064 | tf_op jit(solution)/shard_map/all_gather | solution.py:109
  8.9 128.5 %all-gather.10.cloned.1.call-start = ((), (), s32[]{:S(2)}) async-start(), calls=%async_computation.7 | async-start | bytes 2621440 | tf_op jit(solution)/shard_map/all_gather | solution.py:120
  90.0 1.7 copy-start.8
  92.1 3.8 copy-start.14
  92.7 3.8 copy-start.12
  93.6 89.6 %all-gather.16.cloned.1.call-start = ((), (), s32[]{:S(2)}) async-start(), calls=%async_computation.15 | async-start | bytes 2621440 | tf_op jit(solution)/shard_map/all_gather | solution.py:121
  95.8 146.2 %all-gather.12.cloned.1.call-start = ((), (), s32[]{:S(2)}) async-start(), calls=%async_computation.8 | async-start | bytes 2162688 | tf_op jit(solution)/shard_map/all_gather | solution.py:110
  96.5 302.2 %all-gather.14.cloned.1.call-start = ((), (), s32[]{:S(2)}) async-start(), calls=%async_computation.9 | async-start | bytes 25952256 | tf_op jit(solution)/shard_map/all_gather | solution.py:148
  97.6 513.2 %reduce-scatter.9.cloned.1.call-start = ((), (), s32[]{:S(2)}) async-start(), calls=%async_computation.10 | async-start | bytes 2621440 | tf_op jit(solution)/shard_map/reduce_scatter | solution.py:197
  189.3 52.7 %copy-start = (f32[1,256,1024]{2,1,0:T(8,128)S(1)}, f32[1,256,1024]{2,1,0:T(8,128)}, u32[]{:S(2)}) copy-start(f32[1,256,1024]{2,1,0:T(8,128)} %param.11) | copy-start | bytes 3145732
  239.3 5.4 copy-start.4
  244.9 159.6 %copy-start.2 = (bf16[256,1024]{1,0:T(8,128)(2,1)}, bf16[256,1024]{1,0:T(8,128)(2,1)S(1)}, u32[]{:S(2)}) copy-start(bf16[256,1024]{1,0:T(8,128)(2,1)S(1)} %add_convert_fusion) | copy-start | bytes 1572868
  404.5 5.9 copy-start.5
  417.8 7.3 copy-start.9
  417.8 7.3 copy-start.11
  430.4 1.6 copy-start.1
  568.6 87.8 %reduce-scatter.11.cloned.1.call-start = ((), (), s32[]{:S(2)}) async-start(), calls=%async_computation.11 | async-start | bytes 2621440 | tf_op jit(solution)/shard_map/reduce_scatter | solution.py:200
  572.6 225.0 %reduce-scatter.19.cloned.1.call-start = ((), (), s32[]{:S(2)}) async-start(), calls=%async_computation.16 | async-start | bytes 540672
  663.8 280.8 %reduce-scatter.15.cloned.1.call-start = ((), (), s32[]{:S(2)}) async-start(), calls=%async_computation.13 | async-start | bytes 4325376 | tf_op jit(solution)/shard_map/reduce_scatter | solution.py:225
  667.6 550.9 %reduce-scatter.13.cloned.1.call-start = ((), (), s32[]{:S(2)}) async-start(), calls=%async_computation.12 | async-start | bytes 12976128 | tf_op jit(solution)/shard_map/reduce_scatter | solution.py:224
  675.5 1602.7 %reduce-scatter.17.cloned.1.call-start = ((), (), s32[]{:S(2)}) async-start(), calls=%async_computation.14 | async-start | bytes 51904512 | tf_op jit(solution)/shard_map/reduce_scatter | solution.py:153
  675.8 9.9 copy-start.3
  675.8 9.9 copy-start.10
  685.7 8.2 copy-start.6
  685.7 8.2 copy-start.7
  736.2 7.4 copy-start.13
Sparse Core Ops, SparseCore 0:
  11.6 71.8 all-gather.7
  93.7 43.6 all-gather.9
  139.0 44.1 all-gather.15
  186.6 55.3 all-gather.11
  245.4 153.3 all-gather.13
  568.7 42.0 reduce-scatter.8
  613.2 43.1 reduce-scatter.10
  663.9 133.6 reduce-scatter.18
  800.6 143.9 reduce-scatter.14
  947.4 271.0 reduce-scatter.12
  1221.5 1056.6 reduce-scatter.16
where the time goes:
time: 2290 us; the launch traced here: 2280 us
  waiting for transfers between devices  1840 us (80%)
  matrix products  265 us (12%)
  blocking collectives  70.3 us (3%)
  other arithmetic  60 us (3%)
  local copies, waits for them, and re-layouts  32 us (1%)
    reduce_scatter x1, waiting for transfers between devices, body(): lax.psum_scatter(make_terms(kept_hidden, kept_gate, kept_up, normed2_low,...  1060 us
    reduce_scatter x1, waiting for transfers between devices, body(): lax.psum_scatter(d_qkv_weight, ('dp', 'seq'), scatter_dimension=0, tiled=...  274 us
    all_gather x1, waiting for transfers between devices, body(): lax.all_gather(ffn_low, ('dp', 'seq'), axis=0, tiled=True)  154 us
    reduce_scatter x1, waiting for transfers between devices, body(): lax.psum_scatter(d_out_weight, ('dp', 'seq'), scatter_dimension=0, tiled=...  146 us
    all_gather x1, blocking collectives, body(): lax.all_gather(masters[0], ('dp', 'seq'), axis=1, tiled=True)  70.3 us
    unnamed x12, waiting for transfers between devices  52.9 us
    dot_general x32, matrix products, head_scores(): jnp.einsum('qd,kd->qk', q_head, k_head, preferred_element_type=jnp.float32)  47 us
  transfers between devices with their start and end apart: 11, of which 10 were waited for; matrix products, arithmetic and copies ran while one was open for 7% of the time, Pallas kernels for 0%

commit v1 on v0

v1 whole, which is shorter than its diff:
```python
import functools
import math

import jax
import jax.numpy as jnp
from jax import lax
from jax.experimental import pallas as pl
from jax.experimental.pallas import tpu as pltpu
from jax.sharding import PartitionSpec as P

HEAD_DIM = 64
GROUP = 8
LANES = 128
BF = jnp.bfloat16
F32 = jnp.float32
MESH = pl.DeviceIdType.MESH
NT = (((1,), (1,)), ((), ()))
NN = (((1,), (0,)), ((), ()))
TN = (((0,), (0,)), ((), ()))
EPS = 1e-05


def dot(a, b, dims):
    return lax.dot_general(a, b, dims, preferred_element_type=F32)


def remote(src, dst, send, recv, device):
    return pltpu.make_async_remote_copy(
        src_ref=src, dst_ref=dst, send_sem=send, recv_sem=recv, device_id=device, device_id_type=MESH
    )


def local(src, dst, sem):
    return pltpu.make_async_copy(src, dst, sem)


def greet(peers):
    barrier = pltpu.get_barrier_semaphore()
    for peer in peers:
        pl.semaphore_signal(barrier, inc=1, device_id=peer, device_id_type=MESH)
    pl.semaphore_wait(barrier, len(peers))


def greet_all(dp, seq):
    barrier = pltpu.get_barrier_semaphore()
    total = dp * seq
    me = lax.axis_index("dp") * seq + lax.axis_index("seq")

    def hello(j, carry):
        other = lax.rem(me + j, total)
        pl.semaphore_signal(
            barrier, inc=1, device_id=(other // seq, lax.rem(other, seq)), device_id_type=MESH
        )
        return carry

    lax.fori_loop(1, total, hello, 0)
    pl.semaphore_wait(barrier, total - 1)


class Place:
    def __init__(self, dp, seq):
        self.dp, self.seq = dp, seq
        self.d, self.s = lax.axis_index("dp"), lax.axis_index("seq")
        self.c, self.k = self.d // 2, lax.rem(self.d, 2)
        self.sib = self.d + 1 - 2 * self.k
        self.chips = dp // 2
        self.group = min(dp, GROUP)
        self.groups = dp // self.group
        self.g, self.p = self.d // self.group, lax.rem(self.d, self.group)
        self.gc = self.p // 2
        self.gchips = self.group // 2
        self.half = seq // 2
        self.r, self.h = self.s // self.half, lax.rem(self.s, self.half)
        self.hg = 2 * self.h + self.k
        self.n = self.d * seq + self.s
        self.total = dp * seq

    def in_group(self, chip, core):
        return self.g * self.group + 2 * chip + core


def normalise(value):
    mean = jnp.mean(value, axis=-1, keepdims=True)
    centred = value - mean
    var = jnp.mean(centred * centred, axis=-1, keepdims=True)
    scale = lax.rsqrt(var + EPS)
    return centred * scale, scale


def norm_back(grad, normal, scale, gain):
    scaled = grad * gain
    return scale * (
        scaled
        - jnp.mean(scaled, axis=-1, keepdims=True)
        - normal * jnp.mean(scaled * normal, axis=-1, keepdims=True)
    )


def gather_kernel(
    dp,
    seq,
    tok,
    lnb,
    lens,
    wq,
    wo,
    cot,
    xrow,
    wq_full,
    wo_full,
    ln_out,
    lens_pair,
    dyb_all,
    ln_all,
    wcol,
    xown,
    dyb,
    ln_sem,
    len_sem,
    loc,
    wq1s,
    wq1r,
    wq2s,
    wq2r,
    wo1s,
    wo1r,
    wo2s,
    wo2r,
    wo3s,
    wo3r,
    xs,
    xr,
    xfs,
    xfr,
    dys,
    dyr,
    dyfs,
    dyfr,
):
    me = Place(dp, seq)
    count, width = tok.shape
    wr = wo.shape[0]
    cr = wr * seq
    pair = wcol.shape[2]
    head = pair // 2
    halfrows = count // 2
    dyb[...] = cot[...].astype(BF)
    ln_all[me.n] = lnb[...]
    lens_pair[me.k] = lens[...]
    greet_all(dp, seq)

    def send_ln(j, carry):
        other = lax.rem(me.n + j, me.total)
        remote(
            lnb, ln_all.at[me.n], ln_sem.at[0], ln_sem.at[1], (other // seq, lax.rem(other, seq))
        ).start()
        return carry

    lax.fori_loop(1, me.total, send_ln, 0)
    len_copy = remote(
        lens, lens_pair.at[me.k], len_sem.at[0], len_sem.at[1], (me.sib, me.s)
    )
    len_copy.start()
    row0 = pl.multiple_of(me.s * wr, wr)
    out0 = pl.multiple_of(me.n * wr, wr)
    wq_first, wo_first = [], []
    for j in range(1, seq):
        to = lax.rem(me.s + j, seq)
        col = pl.multiple_of(lax.rem(to, me.half) * pair, pair)
        wq_first.append(
            remote(
                wq.at[:, :, pl.ds(col, pair)],
                wcol.at[:, pl.ds(row0, wr), :],
                wq1s.at[j],
                wq1r.at[j],
                (me.d, to),
            )
        )
    for copy in wq_first:
        copy.start()
    own_col = pl.multiple_of(me.h * pair, pair)
    own_wq = local(wq.at[:, :, pl.ds(own_col, pair)], wcol.at[:, pl.ds(row0, wr), :], loc.at[0])
    own_wq.start()
    own_wo = local(wo, wo_full.at[pl.ds(out0, wr), :], loc.at[1])
    own_wo.start()
    own_dy = local(dyb, dyb_all.at[me.p], loc.at[2])
    own_dy.start()
    normal, _ = normalise(tok[...])
    remote(
        ln_all.at[pl.ds(0, me.total - 1)],
        ln_all.at[pl.ds(0, me.total - 1)],
        ln_sem.at[0],
        ln_sem.at[1],
        (me.sib, me.s),
    ).wait()
    tiles = width // LANES
    per = me.total // tiles
    for t in range(tiles):
        part = ln_all[t * per]
        for i in range(1, per):
            part = part + ln_all[t * per + i]
        ln_out[:, t * LANES : (t + 1) * LANES] = part
    xown[...] = (normal * ln_out[0:1, :] + ln_out[1:2, :]).astype(BF)
    rows0 = pl.multiple_of(me.s * count, count)
    for j in range(me.half):
        to = me.k * me.half + lax.rem(me.h + j, me.half)
        for core in range(2):
            src = xown.at[pl.ds(core * halfrows, halfrows), :]
            dst = xrow.at[pl.ds(rows0 + core * halfrows, halfrows), :]
            here = jnp.logical_and(to == me.s, core == me.k)

            @pl.when(jnp.logical_not(here))
            def _(src=src, dst=dst, core=core, to=to, j=j):
                remote(src, dst, xs.at[j, core], xr.at[me.s], (2 * me.c + core, to)).start()

            @pl.when(here)
            def _(src=src, dst=dst):
                local(src, dst, xr.at[me.s]).start()

    for j in range(1, seq):
        to = lax.rem(me.s + j, seq)
        wo_first.append(
            remote(wo, wo_full.at[pl.ds(out0, wr), :], wo1s.at[j], wo1r.at[j], (me.d, to))
        )
    for copy in wo_first:
        copy.start()
    for copy in wq_first:
        copy.wait()
    own_wq.wait()
    crow0 = pl.multiple_of(me.d * cr, cr)

    def send_wq(j, carry):
        to = lax.rem(me.d + j, dp)
        col = pl.multiple_of(lax.rem(to, 2) * head, head)
        remote(
            wcol.at[:, :, pl.ds(col, head)],
            wq_full.at[:, pl.ds(crow0, cr), :],
            wq2s.at[j],
            wq2r.at[j],
            (to, me.s),
        ).start()
        return carry

    lax.fori_loop(1, dp, send_wq, 0)
    own_half = local(
        wcol.at[:, :, pl.ds(pl.multiple_of(me.k * head, head), head)],
        wq_full.at[:, pl.ds(crow0, cr), :],
        loc.at[3],
    )
    own_half.start()
    for copy in wo_first:
        copy.wait()
    own_wo.wait()
    mine = wo_full.at[pl.ds(crow0, cr), :]
    wo_sends = [remote(mine, mine, wo3s.at[0], wo3r.at[0], (me.sib, me.s))]
    for j in range(1, me.chips):
        to = 2 * lax.rem(me.c + j, me.chips) + me.k
        wo_sends.append(remote(mine, mine, wo2s.at[j], wo2r.at[j], (to, me.s)))
    dy_sends = [remote(dyb, dyb_all.at[me.p], dyfs.at[0], dyfr.at[0], (me.sib, me.s))]
    for j in range(1, me.gchips):
        to = me.in_group(lax.rem(me.gc + j, me.gchips), me.k)
        dy_sends.append(remote(dyb, dyb_all.at[me.p], dys.at[j], dyr.at[j], (to, me.s)))
    for copy in wo_sends + dy_sends:
        copy.start()
    for j in range(seq):
        source = lax.rem(me.s + j, seq)
        part = xrow.at[pl.ds(pl.multiple_of(source * count + me.k * halfrows, halfrows), halfrows), :]
        local(part, part, xr.at[source]).wait()
        remote(part, part, xfs.at[j], xfr.at[j], (me.sib, me.s)).start()
    for j in range(1, me.chips):
        source = 2 * lax.rem(me.c + me.chips - j, me.chips) + me.k
        part = wo_full.at[pl.ds(pl.multiple_of(source * cr, cr), cr), :]
        remote(part, part, wo2s.at[j], wo2r.at[j], (me.sib, me.s)).wait_recv()
        remote(part, part, wo3s.at[j], wo3r.at[j], (me.sib, me.s)).start()
    for j in range(1, me.gchips):
        source = 2 * lax.rem(me.gc + me.gchips - j, me.gchips) + me.k
        part = dyb_all.at[source]
        remote(part, part, dys.at[j], dyr.at[j], (me.sib, me.s)).wait_recv()
        remote(part, part, dyfs.at[j], dyfr.at[j], (me.sib, me.s)).start()
    for j in range(me.half):
        to = me.k * me.half + lax.rem(me.h + j, me.half)
        for core in range(2):
            src = xown.at[pl.ds(core * halfrows, halfrows), :]
            here = jnp.logical_and(to == me.s, core == me.k)

            @pl.when(jnp.logical_not(here))
            def _(src=src, j=j, core=core):
                remote(src, src, xs.at[j, core], xr.at[0], (me.sib, me.s)).wait_send()

    for j in range(seq):
        part = xrow.at[pl.ds(0, halfrows), :]
        remote(part, part, xfs.at[j], xfr.at[j], (me.sib, me.s)).wait()

    def wait_wq(j, carry):
        part = wq_full.at[:, pl.ds(0, cr), :]
        remote(part, part, wq2s.at[j], wq2r.at[j], (me.sib, me.s)).wait()
        return carry

    lax.fori_loop(1, dp, wait_wq, 0)
    own_half.wait()
    own_dy.wait()
    len_copy.wait()
    for j in range(1, me.chips):
        remote(mine, mine, wo2s.at[j], wo2r.at[j], (me.sib, me.s)).wait_send()
        remote(mine, mine, wo3s.at[j], wo3r.at[j], (me.sib, me.s)).wait()
    remote(mine, mine, wo3s.at[0], wo3r.at[0], (me.sib, me.s)).wait()
    for j in range(1, me.gchips):
        remote(dyb, dyb, dys.at[j], dyr.at[j], (me.sib, me.s)).wait_send()
        remote(dyb, dyb, dyfs.at[j], dyfr.at[j], (me.sib, me.s)).wait()
    remote(dyb, dyb, dyfs.at[0], dyfr.at[0], (me.sib, me.s)).wait()


def swap_halves(value):
    half = HEAD_DIM // 2
    width = value.shape[1]
    lane = lax.broadcasted_iota(jnp.int32, value.shape, 1)
    up = pltpu.roll(value, width - half, 1)
    down = pltpu.roll(value, half, 1)
    return jnp.where(lax.rem(lane, HEAD_DIM) < half, up, down)


def head_mask(shape, h):
    lane = lax.broadcasted_iota(jnp.int32, shape, 1)
    return jnp.logical_and(lane >= h * HEAD_DIM, lane < (h + 1) * HEAD_DIM)


def attend_kernel(
    dp,
    seq,
    segs,
    xrow,
    wq,
    lens,
    wf,
    q_out,
    k_out,
    v_out,
    lse_out,
    cos_out,
    sin_out,
    seg_col,
    seg_row,
    mixed_in,
    wf_full,
    mixed,
    ms,
    mr,
    fs,
    fr,
    loc,
):
    me = Place(dp, seq)
    total = xrow.shape[0]
    count = total // seq
    width = wq.shape[2]
    heads = width // HEAD_DIM
    units = wf.shape[1]
    slots = me.groups * seq
    slot = me.g * seq + me.s
    greet_all(dp, seq)
    mine = wf_full.at[:, pl.ds(pl.multiple_of(slot * units, units), units), :]
    own_wf = local(wf, mine, loc.at[0])
    own_wf.start()
    for j in range(1, slots):
        other = lax.rem(slot + j, slots)
        to = ((other // seq) * me.group + me.p, lax.rem(other, seq))
        remote(wf, mine, fs.at[j], fr.at[j], to).start()
    row = lens[me.r]
    place_row = lax.broadcasted_iota(jnp.int32, (8, total), 1)
    place_col = lax.broadcasted_iota(jnp.int32, (total, LANES), 0)
    end = jnp.zeros((1, 1), jnp.int32)
    segr = jnp.zeros((8, total), jnp.int32)
    segc = jnp.zeros((total, LANES), jnp.int32)
    start = jnp.zeros((total, LANES), jnp.int32)
    for j in range(segs):
        length = row[0:1, j : j + 1]
        end = end + length
        segr = segr + (place_row >= end).astype(jnp.int32)
        past = place_col >= end
        segc = segc + past.astype(jnp.int32)
        start = start + jnp.where(past, length, 0)
    seg_row[...] = segr
    seg_col[...] = segc
    half = HEAD_DIM // 2
    lane = lax.broadcasted_iota(jnp.int32, (1, LANES), 1)
    rate = jnp.exp(lax.rem(lane, half).astype(F32) * (-math.log(10000.0) / half))
    angle = (place_col - start).astype(F32) * rate
    cos_out[...] = jnp.cos(angle)
    sign = jnp.where(lax.rem(lane, HEAD_DIM) < half, -1.0, 1.0)
    sin_out[...] = jnp.sin(angle) * sign

    def project(i, carry):
        rows = pl.ds(pl.multiple_of(i * count, count), count)
        x = xrow[rows, :]
        cosine = jnp.concatenate([cos_out[rows, :]] * (width // LANES), axis=1)
        sine = jnp.concatenate([sin_out[rows, :]] * (width // LANES), axis=1)
        raw = dot(x, wq[0], NN)
        q_out[rows, :] = (raw * cosine + swap_halves(raw) * sine).astype(BF)
        raw = dot(x, wq[1], NN)
        k_out[rows, :] = (raw * cosine + swap_halves(raw) * sine).astype(BF)
        v_out[rows, :] = dot(x, wq[2], NN).astype(BF)
        return carry

    lax.fori_loop(0, seq, project, 0)

    def chunk(step, carry):
        i = lax.rem(me.s + step, seq)
        rows = pl.ds(pl.multiple_of(i * count, count), count)
        q = q_out[rows, :]
        bias = jnp.where(seg_col[rows, 0:1] == seg_row[0:1, :], 0.0, -1e30)
        lane = lax.broadcasted_iota(jnp.int32, (count, LANES), 1)
        lse = jnp.zeros((count, LANES), F32)
        out = jnp.zeros((count, width), F32)
        for h in range(heads):
            mask = head_mask((count, width), h)
            score = dot(jnp.where(mask, q, jnp.zeros_like(q)), k_out[...], NT) * 0.125 + bias
            top = jnp.max(score, axis=1, keepdims=True)
            weight = jnp.exp(score - top)
            tally = jnp.sum(weight, axis=1, keepdims=True)
            prob = (weight * (1.0 / tally)).astype(BF)
            out = jnp.where(mask, dot(prob, v_out[...], NN), out)
            lse = jnp.where(lane == h, top + jnp.log(tally), lse)
        lse_out[rows, :] = lse
        mixed[i] = out.astype(BF)
        owner = 2 * me.c + me.r
        here = jnp.logical_and(i == me.s, owner == me.d)

        @pl.when(jnp.logical_not(here))
        def _():
            remote(mixed.at[i], mixed_in.at[me.hg], ms.at[i], mr.at[me.hg], (owner, i)).start()

        @pl.when(here)
        def _():
            local(mixed.at[i], mixed_in.at[me.hg], mr.at[me.hg]).start()

        return carry

    lax.fori_loop(0, seq, chunk, 0)
    for j in range(seq):
        local(mixed.at[j], mixed_in.at[j], mr.at[j]).wait()
        here = jnp.logical_and(j == me.s, me.r == me.k)

        @pl.when(jnp.logical_not(here))
        def _(j=j):
            remote(mixed.at[j], mixed.at[j], ms.at[j], mr.at[j], (me.sib, me.s)).wait_send()

    own_wf.wait()
    for j in range(1, slots):
        remote(wf, mine, fs.at[j], fr.at[j], (me.sib, me.s)).wait()


def ffn_kernel(
    dp,
    seq,
    tok,
    mixed_in,
    wo,
    ln,
    dyb_all,
    wf,
    cot,
    mid_out,
    dmid_out,
    ln2_out,
    br_out,
    gf_out,
    xn2,
    xall,
    hid,
    dg,
    du,
    dpart,
    dsib,
    dsum,
    drecv,
    bpart,
    bsib,
    normal2,
    scale2,
    loc,
    xs,
    xr,
    xfs,
    xfr,
    dss,
    dsr,
    dps,
    dpr,
    bss,
    bsr,
):
    me = Place(dp, seq)
    count, width = tok.shape
    units = wf.shape[1]
    nc = me.gchips
    tile = min(256, units)
    cols = 256
    sib = (me.sib, me.s)
    mid = tok[...]
    block = mixed_in.shape[2]
    for h in range(mixed_in.shape[0]):
        mid = mid + dot(mixed_in[h], wo[h * block : (h + 1) * block, :], NN)
    mid_out[...] = mid
    normal, scale = normalise(mid)
    normal2[...] = normal
    scale2[...] = jnp.broadcast_to(scale, scale2.shape)
    low = (normal * ln[2:3, :] + ln[3:4, :]).astype(BF)
    xn2[...] = low
    greet([sib] + [(me.in_group(lax.rem(me.gc + j, nc), me.k), me.s) for j in range(1, nc)])
    sends = [remote(xn2, xall.at[me.gc, me.k], xfs.at[0], xfr.at[0], sib)]
    for j in range(1, nc):
        to = me.in_group(lax.rem(me.gc + j, nc), me.k)
        sends.append(remote(xn2, xall.at[me.gc, me.k], xs.at[j], xr.at[j], (to, me.s)))
    for copy in sends:
        copy.start()
    xall[me.gc, me.k] = low

    def chip(j, carry):
        cj = lax.rem(me.gc + nc - j, nc)

        @pl.when(j > 0)
        def _():
            part = xall.at[cj, me.k]
            remote(part, part, xs.at[j], xr.at[j], sib).wait_recv()
            remote(part, part, xfs.at[j], xfr.at[j], sib).start()

        theirs = xall.at[cj, 1 - me.k]
        remote(theirs, theirs, xfs.at[j], xfr.at[j], sib).wait_recv()
        rows = pl.ds(pl.multiple_of(cj * 2 * count, 2 * count), 2 * count)
        x = xall[cj].reshape(2 * count, width)
        dy = dyb_all[pl.ds(2 * cj, 2)].reshape(2 * count, width)
        for t in range(units // tile):
            span = slice(t * tile, (t + 1) * tile)
            gate = dot(x, wf[0, span, :], NT)
            up = dot(x, wf[1, span, :], NT)
            dh = dot(dy, wf[2, span, :], NT)
            sigma = 1.0 / (1.0 + jnp.exp(-gate))
            active = gate * sigma
            hid[rows, span] = (active * up).astype(BF)
            dg[rows, span] = (dh * up * (sigma * (1.0 + gate * (1.0 - sigma)))).astype(BF)
            du[rows, span] = (dh * active).astype(BF)
        for t in range(width // cols):
            span = slice(t * cols, (t + 1) * cols)
            value = dot(dg[rows, :], wf[0, :, span], NN) + dot(du[rows, :], wf[1, :, span], NN)
            dpart[j, :, :, span] = value.astype(BF).reshape(2, count, cols)
        remote(dpart.at[j, 1 - me.k], dsib.at[j], dss.at[j], dsr.at[j], sib).start()
        for t in range(width // cols):
            span = slice(t * cols, (t + 1) * cols)
            value = dot(hid[rows, :], wf[2, :, span], NN)
            bpart[j, :, :, span] = value.astype(BF).reshape(2, count, cols)
        remote(bpart.at[j, 1 - me.k], bsib.at[j], bss.at[j], bsr.at[j], sib).start()
        remote(dsib.at[j], dsib.at[j], dss.at[j], dsr.at[j], sib).wait()
        dsum[j] = (dpart[j, me.k].astype(F32) + dsib[j].astype(F32)).astype(BF)

        @pl.when(j > 0)
        def _():
            remote(
                dsum.at[j], drecv.at[j], dps.at[j], dpr.at[j], (me.in_group(cj, me.k), me.s)
            ).start()

        return carry

    lax.fori_loop(0, nc, chip, 0)

    def grads(t, carry):
        span = pl.ds(pl.multiple_of(t * tile, tile), tile)
        x = xall[...].reshape(nc * 2 * count, width)
        dy = dyb_all[...].reshape(nc * 2 * count, width)
        gf_out[0, span, :] = dot(dg[:, span], x, TN).astype(BF)
        gf_out[1, span, :] = dot(du[:, span], x, TN).astype(BF)
        gf_out[2, span, :] = dot(hid[:, span], dy, TN).astype(BF)
        return carry

    lax.fori_loop(0, units // tile, grads, 0)
    for j in range(nc):
        remote(bsib.at[j], bsib.at[j], bss.at[j], bsr.at[j], sib).wait()
        br_out[j] = (bpart[j, me.k].astype(F32) + bsib[j].astype(F32)).astype(BF)
        remote(xn2, xn2, xfs.at[j], xfr.at[j], sib).wait_send()
    dn2 = dsum[0].astype(F32)
    for j in range(1, nc):
        remote(dsum.at[j], drecv.at[j], dps.at[j], dpr.at[j], sib).wait()
        remote(xn2, xn2, xs.at[j], xr.at[j], sib).wait_send()
        dn2 = dn2 + drecv[j].astype(F32)
    normal = normal2[...]
    dmid_out[...] = cot[...] + norm_back(dn2, normal, scale2[:, 0:1], ln[2:3, :])
    ln2_out[0:1, :] = jnp.sum(dn2 * normal, axis=0, keepdims=True)
    ln2_out[1:2, :] = jnp.sum(dn2, axis=0, keepdims=True)
    ln2_out[2:8, :] = jnp.zeros((6, width), F32)


def back_kernel(
    dp,
    seq,
    tok,
    mid,
    dmid,
    ln,
    ln2,
    brsum,
    gf,
    mixed_in,
    wo,
    wq,
    xrow,
    q_in,
    k_in,
    v_in,
    lse_in,
    cos_in,
    sin_in,
    seg_col,
    seg_row,
    out,
    input_grad,
    lng,
    qg,
    og,
    fg,
    dmix,
    dmix_row,
    brr,
    ogp,
    ogsib,
    ogs,
    ogpl,
    ogc,
    ogz,
    dq,
    dk,
    dv,
    dnp,
    dnsib,
    dns,
    dnr,
    qgp,
    qgt,
    qgpl,
    qgc,
    qgz,
    fgr,
    lnp,
    lnr,
    loc,
    dms,
    dmr,
    brs,
    brrs,
    gs,
    gr,
    o1,
    o2s,
    o2r,
    o3s,
    o3r,
    n1,
    n2s,
    n2r,
    q1s,
    q1r,
    q2s,
    q2r,
    lnsem,
):
    me = Place(dp, seq)
    count, width = tok.shape
    total = xrow.shape[0]
    block = q_in.shape[1]
    heads = block // HEAD_DIM
    wr = og.shape[0]
    cr = wr * seq
    units = fg.shape[1]
    slots = me.groups * seq
    slot = me.g * seq + me.s
    sib = (me.sib, me.s)
    greet_all(dp, seq)
    dmb = dmid[...].astype(BF)
    for hg in range(seq):
        dmix[hg] = dot(dmb, wo[hg * block : (hg + 1) * block, :], NT).astype(BF)
        to = (2 * me.c + hg % 2, me.k * me.half + hg // 2)
        here = jnp.logical_and(to[0] == me.d, to[1] == me.s)
        src, dst = dmix.at[hg], dmix_row.at[me.s]

        @pl.when(jnp.logical_not(here))
        def _(src=src, dst=dst, hg=hg, to=to):
            remote(src, dst, dms.at[hg], dmr.at[me.s], to).start()

        @pl.when(here)
        def _(src=src, dst=dst):
            local(src, dst, dmr.at[me.s]).start()

    for j in range(1, me.gchips):
        to = me.in_group(lax.rem(me.gc + me.gchips - j, me.gchips), me.k)
        remote(brsum.at[j], brr.at[j], brs.at[j], brrs.at[j], (to, me.s)).start()
    for j in range(1, slots):
        other = lax.rem(slot + j, slots)
        to = ((other // seq) * me.group + me.p, lax.rem(other, seq))
        src = gf.at[:, pl.ds(pl.multiple_of(other * units, units), units), :]
        remote(src, fgr.at[j], gs.at[j], gr.at[j], to).start()
    for h in range(seq):
        part = dot(mixed_in[h], dmb, TN).astype(BF)
        for t in range(block // cr):
            first = h * (block // cr) + t
            ogp[first % 2, first // 2] = part[t * cr : (t + 1) * cr]
    remote(ogp.at[1 - me.k], ogsib, o1.at[0], o1.at[1], sib).start()
    for j in range(seq):
        local(dmix.at[j], dmix_row.at[j], dmr.at[j]).wait()
    remote(ogp.at[1 - me.k], ogsib, o1.at[0], o1.at[1], sib).wait()
    ogs[...] = (ogp[me.k].astype(F32) + ogsib[...].astype(F32)).astype(BF)

    def send_og(j, carry):
        chip = lax.rem(me.c + j, me.chips)
        remote(ogs.at[chip], ogpl.at[j], o2s.at[j], o2r.at[j], (2 * chip + me.k, me.s)).start()
        return carry

    lax.fori_loop(1, me.chips, send_og, 0)
    dk[...] = jnp.zeros_like(dk)
    dv[...] = jnp.zeros_like(dv)

    def chunk(i, carry):
        rows = pl.ds(pl.multiple_of(i * count, count), count)
        q = q_in[rows, :]
        dm = dmix_row[i]
        lse = lse_in[rows, :]
        bias = jnp.where(seg_col[rows, 0:1] == seg_row[0:1, :], 0.0, -1e30)
        grad_q = jnp.zeros((count, block), F32)
        for h in range(heads):
            mask = head_mask((count, block), h)
            qh = jnp.where(mask, q, jnp.zeros_like(q))
            dmh = jnp.where(mask, dm, jnp.zeros_like(dm))
            score = dot(qh, k_in[...], NT) * 0.125 + bias
            prob = jnp.exp(score - lse[:, h : h + 1])
            dprob = dot(dmh, v_in[...], NT)
            centre = jnp.sum(prob * dprob, axis=1, keepdims=True)
            ds = (0.125 * prob * (dprob - centre)).astype(BF)
            grad_q = jnp.where(mask, dot(ds, k_in[...], NN), grad_q)
            dk[...] += dot(ds, qh, TN)
            dv[...] += dot(prob.astype(BF), dmh, TN)
        dq[rows, :] = grad_q
        return carry

    lax.fori_loop(0, seq, chunk, 0)

    def back_chunk(i):
        rows = pl.ds(pl.multiple_of(i * count, count), count)
        cosine = jnp.concatenate([cos_in[rows, :]] * (block // LANES), axis=1)
        sine = jnp.concatenate([sin_in[rows, :]] * (block // LANES), axis=1)
        a = dq[rows, :]
        a = (a * cosine - swap_halves(a) * sine).astype(BF)
        b = dk[rows, :]
        b = (b * cosine - swap_halves(b) * sine).astype(BF)
        c = dv[rows, :].astype(BF)
        qgp[0, rows, :] = a
        qgp[1, rows, :] = b
        qgp[2, rows, :] = c
        value = dot(a, wq[0], NT) + dot(b, wq[1], NT) + dot(c, wq[2], NT)
        dnp[lax.rem(i, 2), i // 2] = value.astype(BF)

    def other_half(j, carry):
        back_chunk(2 * j + 1 - me.k)
        return carry

    def own_half(j, carry):
        back_chunk(2 * j + me.k)
        return carry

    lax.fori_loop(0, me.half, other_half, 0)
    remote(dnp.at[1 - me.k], dnsib, n1.at[0], n1.at[1], sib).start()
    lax.fori_loop(0, me.half, own_half, 0)
    remote(dnp.at[1 - me.k], dnsib, n1.at[0], n1.at[1], sib).wait()
    owner = 2 * me.c + me.r
    for j in range(me.half):
        dns[j] = (dnp[me.k, j].astype(F32) + dnsib[j].astype(F32)).astype(BF)
        i = 2 * j + me.k
        here = jnp.logical_and(owner == me.d, i == me.s)

        @pl.when(jnp.logical_not(here))
        def _(j=j, i=i):
            remote(dns.at[j], dnr.at[me.h], n2s.at[j], n2r.at[me.h], (owner, i)).start()

        @pl.when(here)
        def _(j=j):
            local(dns.at[j], dnr.at[me.h], n2r.at[me.h]).start()

    acc = ogs[me.c].astype(F32)
    for j in range(1, me.chips):
        remote(ogs.at[0], ogpl.at[j], o2s.at[j], o2r.at[j], sib).wait()
        acc = acc + ogpl[j].astype(F32)
    ogc[...] = acc.astype(BF)
    for j in range(1, seq):
        to = lax.rem(me.s + j, seq)
        src = ogc.at[pl.ds(pl.multiple_of(to * wr, wr), wr), :]
        remote(src, ogz.at[j], o3s.at[j], o3r.at[j], (me.d, to)).start()
    span_rows = 2 * cr

    tile_rows = qgt.shape[2]
    per_tile = tile_rows // span_rows

    def qkv_terms(j, carry):
        at = lax.rem(me.c // per_tile + j, width // tile_rows)
        x = xrow[:, pl.ds(pl.multiple_of(at * tile_rows, tile_rows), tile_rows)]
        for t in range(3):
            qgt[at, t] = dot(x, qgp[t], TN).astype(BF)
        for i in range(per_tile):
            chip = at * per_tile + i

            @pl.when(chip != me.c)
            def _(i=i, chip=chip):
                src = qgt.at[at, :, i * span_rows : (i + 1) * span_rows, :]
                to = (2 * chip + me.k, me.s)
                remote(src, qgpl.at[me.c], q1s.at[chip], q1r.at[me.c], to).start()

        return carry

    tiles_of = width // tile_rows
    lax.fori_loop(1, tiles_of, qkv_terms, 0)
    qkv_terms(0, 0)
    own = pl.ds(pl.multiple_of(lax.rem(me.c, per_tile) * span_rows, span_rows), span_rows)
    sums = [qgt[me.c // per_tile, t, own, :].astype(F32) for t in range(3)]
    for j in range(1, me.chips):
        chip = lax.rem(me.c + j, me.chips)
        remote(qgpl.at[chip], qgpl.at[chip], q1s.at[chip], q1r.at[chip], sib).wait()
        for t in range(3):
            sums[t] = sums[t] + qgpl[chip, t].astype(F32)
    for t in range(3):
        qgc[t] = sums[t].astype(BF)
    source = me.k * seq + me.s
    for core in range(2):
        for j in range(seq):
            to = lax.rem(me.s + j, seq)
            src = qgc.at[:, pl.ds(pl.multiple_of((core * seq + to) * wr, wr), wr), :]
            here = jnp.logical_and(core == me.k, to == me.s)

            @pl.when(jnp.logical_not(here))
            def _(src=src, core=core, to=to, j=j):
                remote(
                    src, qgz.at[source], q2s.at[core, j], q2r.at[source], (2 * me.c + core, to)
                ).start()

            @pl.when(here)
            def _(src=src):
                local(src, qgz.at[source], q2r.at[source]).start()

    dn1 = jnp.zeros((count, width), F32)
    for h in range(me.half):
        local(dnr.at[h], dnr.at[h], n2r.at[h]).wait()
        dn1 = dn1 + dnr[h].astype(F32)
    normal, scale = normalise(tok[...])
    input_grad[...] = dmid[...] + norm_back(dn1, normal, scale, ln[0:1, :])
    gain1 = jnp.sum(dn1 * normal, axis=0, keepdims=True)
    shift1 = jnp.sum(dn1, axis=0, keepdims=True)
    tiles = width // LANES
    per = me.total // tiles
    for t in range(tiles):
        lanes = slice(t * LANES, (t + 1) * LANES)
        lnp[t, 0:1, :] = gain1[:, lanes]
        lnp[t, 1:2, :] = shift1[:, lanes]
        lnp[t, 2:4, :] = ln2[0:2, lanes]
        lnp[t, 4:8, :] = ln2[2:6, lanes]

    def send_ln(j, carry):
        other = lax.rem(me.n + j, me.total)
        remote(
            lnp.at[other // per],
            lnr.at[me.n],
            lnsem.at[0],
            lnsem.at[1],
            (other // seq, lax.rem(other, seq)),
        ).start()
        return carry

    lax.fori_loop(1, me.total, send_ln, 0)
    lnr[me.n] = lnp[me.n // per]
    value = mid[...] + brsum[0].astype(F32)
    for j in range(1, me.gchips):
        remote(brsum.at[j], brr.at[j], brs.at[j], brrs.at[j], sib).wait()
        value = value + brr[j].astype(F32)
    out[...] = value
    acc = ogc[pl.ds(pl.multiple_of(me.s * wr, wr), wr), :].astype(F32)
    for j in range(1, seq):
        remote(ogz.at[j], ogz.at[j], o3s.at[j], o3r.at[j], sib).wait()
        acc = acc + ogz[j].astype(F32)
    og[...] = acc
    acc = gf[:, pl.ds(pl.multiple_of(slot * units, units), units), :].astype(F32)
    for j in range(1, slots):
        remote(fgr.at[j], fgr.at[j], gs.at[j], gr.at[j], sib).wait()
        acc = acc + fgr[j].astype(F32)
    fg[...] = acc
    for j in range(2 * seq):
        local(qgz.at[j], qgz.at[j], q2r.at[j]).wait()
    for hg in range(seq):
        core, h = hg % 2, hg // 2
        acc = qgz[core * seq + h].astype(F32)
        for r in range(1, 2):
            acc = acc + qgz[core * seq + r * me.half + h].astype(F32)
        qg[:, :, hg * block : (hg + 1) * block] = acc
    rest = lnr.at[pl.ds(0, me.total - 1)]
    remote(rest, rest, lnsem.at[0], lnsem.at[1], sib).wait()
    acc = lnr[0]
    for j in range(1, me.total):
        acc = acc + lnr[j]
    lng[...] = acc
    for hg in range(seq):
        to = (2 * me.c + hg % 2, me.k * me.half + hg // 2)
        here = jnp.logical_and(to[0] == me.d, to[1] == me.s)

        @pl.when(jnp.logical_not(here))
        def _(hg=hg):
            remote(dmix.at[hg], dmix.at[hg], dms.at[hg], dmr.at[0], sib).wait_send()

    for j in range(me.half):
        here = jnp.logical_and(owner == me.d, 2 * j + me.k == me.s)

        @pl.when(jnp.logical_not(here))
        def _(j=j):
            remote(dns.at[j], dns.at[j], n2s.at[j], n2r.at[0], sib).wait_send()

    for core in range(2):
        for j in range(seq):
            here = jnp.logical_and(core == me.k, j == 0)
            src = qgc.at[:, pl.ds(0, wr), :]

            @pl.when(jnp.logical_not(here))
            def _(src=src, core=core, j=j):
                remote(src, src, q2s.at[core, j], q2r.at[0], sib).wait_send()


def shape(dims, dtype):
    return jax.ShapeDtypeStruct(dims, dtype)


def call(kernel, name, number, operands, outs, scratch, flops):
    vmem = pl.BlockSpec(memory_space=pltpu.VMEM)
    return pl.pallas_call(
        kernel,
        out_shape=tuple(outs),
        in_specs=[vmem] * len(operands),
        out_specs=tuple([vmem] * len(outs)),
        scratch_shapes=scratch,
        compiler_params=pltpu.CompilerParams(
            collective_id=number, has_side_effects=True, vmem_limit_bytes=60 * 2**20
        ),
        cost_estimate=pl.CostEstimate(
            flops=flops, bytes_accessed=2**24, transcendentals=0
        ),
        name=name,
    )(*operands)


def body(dp, seq, tokens, ln_params, qkv_weight, out_weight, ffn_weight, lengths, cotangent):
    count, width = tokens.shape[1], tokens.shape[2]
    ranks = dp * seq
    total = count * seq
    wr = qkv_weight.shape[0]
    units = ffn_weight.shape[0]
    block = width // seq
    group = min(dp, GROUP)
    gchips, chips, slots = group // 2, dp // 2, (dp // group) * seq
    held = units * slots
    share = ln_params.shape[1]
    sem = pltpu.SemaphoreType.DMA
    vm = pltpu.VMEM
    tok = tokens.reshape(count, width)
    cot = cotangent.reshape(count, width)
    rank = lax.axis_index("dp") * seq + lax.axis_index("seq")
    fit = LANES // share
    lane = jnp.arange(LANES)
    gains = jnp.tile(ln_params.astype(BF).astype(F32), (1, fit))
    lnb = jnp.where((lane // share == rank % fit)[None, :], gains, 0.0)
    lnb = jnp.pad(lnb, ((0, 4), (0, 0)))
    lens = jnp.pad(lengths, ((0, 7), (0, LANES - lengths.shape[1])))
    wq = qkv_weight.astype(BF).transpose(1, 0, 2)
    wo = out_weight.astype(BF)
    wf = ffn_weight.astype(BF).transpose(1, 0, 2)

    xrow, wq_full, wo_full, ln, lens_pair, dyb_all = call(
        functools.partial(gather_kernel, dp, seq),
        "gather",
        1,
        (tok, lnb, lens, wq, wo, cot),
        (
            shape((total, width), BF),
            shape((3, width, block), BF),
            shape((width, width), BF),
            shape((8, width), F32),
            shape((2, 8, LANES), jnp.int32),
            shape((group, count, width), BF),
        ),
        [
            vm((ranks, 8, LANES), F32),
            vm((3, wr * seq, 2 * block), BF),
            vm((count, width), BF),
            vm((count, width), BF),
            sem((2,)),
            sem((2,)),
            sem((4,)),
            sem((seq,)),
            sem((seq,)),
            sem((dp,)),
            sem((dp,)),
            sem((seq,)),
            sem((seq,)),
            sem((chips,)),
            sem((chips,)),
            sem((chips,)),
            sem((chips,)),
            sem((seq, 2)),
            sem((seq,)),
            sem((seq,)),
            sem((seq,)),
            sem((gchips,)),
            sem((gchips,)),
            sem((gchips,)),
            sem((gchips,)),
        ],
        10**6,
    )
    q, k, v, lse, cosine, sine, seg_col, seg_row, mixed_in, wf_full = call(
        functools.partial(attend_kernel, dp, seq, lengths.shape[1]),
        "attend",
        2,
        (xrow, wq_full, lens_pair, wf),
        (
            shape((total, block), BF),
            shape((total, block), BF),
            shape((total, block), BF),
            shape((total, LANES), F32),
            shape((total, LANES), F32),
            shape((total, LANES), F32),
            shape((total, LANES), jnp.int32),
            shape((8, total), jnp.int32),
            shape((seq, count, block), BF),
            shape((3, held, width), BF),
        ),
        [
            vm((seq, count, block), BF),
            sem((seq,)),
            sem((seq,)),
            sem((slots,)),
            sem((slots,)),
            sem((1,)),
        ],
        4 * 10**9,
    )
    mid, dmid, ln2, brsum, gf = call(
        functools.partial(ffn_kernel, dp, seq),
        "ffn",
        3,
        (tok, mixed_in, wo_full, ln, dyb_all, wf_full, cot),
        (
            shape((count, width), F32),
            shape((count, width), F32),
            shape((8, width), F32),
            shape((gchips, count, width), BF),
            shape((3, held, width), BF),
        ),
        [
            vm((count, width), BF),
            vm((gchips, 2, count, width), BF),
            vm((group * count, held), BF),
            vm((group * count, held), BF),
            vm((group * count, held), BF),
            vm((gchips, 2, count, width), BF),
            vm((gchips, count, width), BF),
            vm((gchips, count, width), BF),
            vm((gchips, count, width), BF),
            vm((gchips, 2, count, width), BF),
            vm((gchips, count, width), BF),
            vm((count, width), F32),
            vm((count, LANES), F32),
            sem((1,)),
        ]
        + [sem((gchips,))] * 10,
        20 * 10**9,
    )
    out, input_grad, lng, qg, og, fg = call(
        functools.partial(back_kernel, dp, seq),
        "back",
        4,
        (
            tok,
            mid,
            dmid,
            ln,
            ln2,
            brsum,
            gf,
            mixed_in,
            wo_full,
            wq_full,
            xrow,
            q,
            k,
            v,
            lse,
            cosine,
            sine,
            seg_col,
            seg_row,
        ),
        (
            shape((count, width), F32),
            shape((count, width), F32),
            shape((8, LANES), F32),
            shape((3, wr, width), F32),
            shape((wr, width), F32),
            shape((3, units, width), F32),
        ),
        [
            vm((seq, count, block), BF),
            vm((seq, count, block), BF),
            vm((gchips, count, width), BF),
            vm((2, chips, wr * seq, width), BF),
            vm((chips, wr * seq, width), BF),
            vm((chips, wr * seq, width), BF),
            vm((chips, wr * seq, width), BF),
            vm((wr * seq, width), BF),
            vm((seq, wr, width), BF),
            vm((total, block), F32),
            vm((total, block), F32),
            vm((total, block), F32),
            vm((2, seq // 2, count, width), BF),
            vm((seq // 2, count, width), BF),
            vm((seq // 2, count, width), BF),
            vm((seq // 2, count, width), BF),
            vm((3, total, block), BF),
            vm((width // block, 3, block, block), BF),
            vm((chips, 3, 2 * wr * seq, block), BF),
            vm((3, 2 * wr * seq, block), BF),
            vm((2 * seq, 3, wr, block), BF),
            vm((slots, 3, units, width), BF),
            vm((width // LANES, 8, LANES), F32),
            vm((ranks, 8, LANES), F32),
            sem((1,)),
            sem((seq,)),
            sem((seq,)),
            sem((gchips,)),
            sem((gchips,)),
            sem((slots,)),
            sem((slots,)),
            sem((2,)),
            sem((chips,)),
            sem((chips,)),
            sem((seq,)),
            sem((seq,)),
            sem((2,)),
            sem((seq,)),
            sem((seq,)),
            sem((chips,)),
            sem((chips,)),
            sem((2, seq)),
            sem((2 * seq,)),
            sem((2,)),
        ],
        8 * 10**9,
    )
    first = (rank % fit) * share
    ln_grad = lax.dynamic_slice(lng, (0, first), (4, share))
    return (
        out.reshape(1, count, width),
        input_grad.reshape(1, count, width),
        ln_grad,
        qg.transpose(1, 0, 2),
        og,
        fg.transpose(1, 0, 2),
    )


def solution(mesh):
    dp, seq = mesh.shape["dp"], mesh.shape["seq"]
    both = ("dp", "seq")
    in_specs = (
        P("dp", "seq", None),
        P(None, both),
        P(both, None, None),
        P(both, None),
        P(both, None, None),
        P("dp", None),
        P("dp", "seq", None),
    )
    out_specs = (
        P("dp", "seq", None),
        P("dp", "seq", None),
        P(None, both),
        P(both, None, None),
        P(both, None),
        P(both, None, None),
    )
    return jax.shard_map(
        functools.partial(body, dp, seq),
        mesh=mesh,
        in_specs=in_specs,
        out_specs=out_specs,
        check_vma=False,
    )
```

time: 2290 us -> 401 us (0.18)
  waiting for transfers between devices: 1840 us -> 0 us
  Pallas kernels: 0 us -> 384 us
  matrix products: 265 us -> 0 us
  blocking collectives: 70.3 us -> 0 us
  other arithmetic: 60 us -> 6.34 us
    reduce_scatter x5 -> x0, waiting for transfers between devices: 1550 us -> none  [the longest x1 1060 us: body(): lax.psum_scatter(make_terms(kept_hidden, kept_gate, kept_up, normed2_low,...]
    pallas_call x0 -> x4, Pallas kernels: none -> 384 us  [call(): pl.pallas_call(kernel, out_shape=tuple(outs), in_specs=[vmem] * len(opera...]
    dot_general x127 -> x0, matrix products: 265 us -> none  [the longest x32 47 us: head_scores(): jnp.einsum('qd,kd->qk', q_head, k_head, preferred_element_type=jnp.float32)]
    all_gather x5 -> x0, waiting for transfers between devices: 236 us -> none  [the longest x1 154 us: body(): lax.all_gather(ffn_low, ('dp', 'seq'), axis=0, tiled=True)]
    all_gather x1 -> x0, blocking collectives: 70.3 us -> none  [body(): lax.all_gather(masters[0], ('dp', 'seq'), axis=1, tiled=True)]
    unnamed x12 -> x0, waiting for transfers between devices: 52.9 us -> none
    another operation x9 -> x0, other arithmetic: 36.8 us -> none  [the longest x1 34 us: make_terms(): return jnp.stack([gate_term, up_term, down_term], axis=1)]
  transfers between devices with their start and end apart: 11 -> 0, of which waited for: 10 -> 0; matrix products, arithmetic and copies ran while one was open for 7% -> 0% of each run, Pallas kernels for 0% -> 0%
where the time goes in v1:
time: 401 us
  Pallas kernels  384 us (96%)
  local copies, waits for them, and re-layouts  9.25 us (2%)
  other arithmetic  6.34 us (2%)
    pallas_call x4, Pallas kernels, call(): pl.pallas_call(kernel, out_shape=tuple(outs), in_specs=[vmem] * len(opera...  384 us

profile of v1, /device:TPU:0, one launch (start us, length us, event | category | flops | bytes accessed | tf_op | source)
XLA Modules:
  0.0 400.7 jit_solution(7565673177704944086)
XLA Ops:
  0.7 0.7 convert_convert_fusion
  1.3 1.3 pad.9.lens
  2.6 0.1 tile.10
  2.7 0.6 pad.8.lnb
  3.3 1.5 convert_element_type.20.wo
  4.8 1.7 convert_bitcast_fusion.1.wq
  6.5 2.4 convert_bitcast_fusion.wf
  8.9 81.7 %gather.1 = (bf16[1024,1024]{1,0:T(8,128)(2,1)}, bf16[3,1024,256]{2,1,0:T(8,128)(2,1)}, bf16[1024,1024]{1,0:T(8,128)(2,1)}, f32[8,1024]{1,0:T(8,128)}, s32[2,8,1...) custom-call(f32[256,1024]{1,0:T(8,128)} %bitcast.13, f32[8,128]{1,0:T(8,128)} %pad.8.lnb, s32[8,128]{1,0:T(8,128)} %pad.9.lens, ...), custom_call_target="tpu_custom_call" | custom-call | flops 1000000 | bytes 16777216 | tf_op jit(solution)/shard_map/gather/pallas_call | solution.py:933
  90.7 76.3 %attend.1 = (bf16[1024,256]{1,0:T(8,128)(2,1)}, bf16[1024,256]{1,0:T(8,128)(2,1)}, bf16[1024,256]{1,0:T(8,128)(2,1)}, f32[1024,128]{1,0:T(8,128)}, f32[1024,128]...) custom-call(bf16[1024,1024]{1,0:T(8,128)(2,1)} %get-tuple-element.33, ...), custom_call_target="tpu_custom_call" | custom-call | flops 4000000000 | bytes 16777216 | tf_op jit(solution)/shard_map/attend/pallas_call | solution.py:933
  167.0 83.8 %ffn.1 = (f32[256,1024]{1,0:T(8,128)}, f32[256,1024]{1,0:T(8,128)}, f32[8,1024]{1,0:T(8,128)}, bf16[4,256,1024]{2,1,0:T(8,128)(2,1)}, bf16[3,512,1024]{2,1,0:T(8,128)(2,1)}) custom-call(f32[256,1024]{1,0:T(8,128)} %bitcast.14, bf16[4,256,256]{2,1,0:T(8,128)(2,1)} %get-tuple-element.36.mixed_in, bf16[1024,1024]{1,0:T(8,128)(2,1)} %get-tuple-element.37.wo, ...), custom_call_target="tpu_custom_call" | custom-call | flops 20000000000 | bytes 16777216 | tf_op jit(solution)/shard_map/ffn/pallas_call | solution.py:933
  250.8 142.6 %back.1 = (f32[256,1024]{1,0:T(8,128)}, f32[256,1024]{1,0:T(8,128)}, f32[8,128]{1,0:T(8,128)}, f32[3,32,1024]{2,1,0:T(8,128)}, f32[32,1024]{1,0:T(8,128)}, /*index=5*/f32[3,128,1024]{2,1,0:T(8,128)}) custom-call(f32[256,1024]{1,0:T(8,128)} %bitcast.15, f32[256,1024]{1,0:T(8,128)} %get-tuple-element.41.mid, f32[256,1024]{1,0:T(8,128)} %get-tuple-element.42.dmid, ...), custom_call_target="tpu_custom_call" | custom-call | flops 8000000000 | bytes 16777216 | tf_op jit(solution)/shard_map/back/pallas_call | solution.py:933
  393.3 0.0 copy-start.1
  393.3 1.4 constant_dynamic-slice_fusion
  394.8 0.0 copy-start.2
  394.8 0.0 copy-start.3
  394.8 2.4 copy.18
  397.1 0.0 copy-done.1
  397.1 0.0 copy-start
  397.1 1.0 copy.19
  398.1 0.0 copy-done.2
  398.1 0.7 copy.20
  398.8 0.0 copy-done.3
  398.8 0.7 copy.21
  399.5 0.0 copy-done
  399.5 1.1 copy.22
  (3 shorter events, 0.0 us)
Async XLA Ops:
  393.3 3.8 copy-start.1
  394.8 3.3 copy-start.2
  394.8 4.1 %copy-start.3 = (f32[32,1024]{1,0:T(8,128)S(1)}, f32[32,1024]{1,0:T(8,128)}, u32[]{:S(2)}) copy-start(f32[32,1024]{1,0:T(8,128)} %get-tuple-element.70) | copy-start | bytes 393220
  397.1 2.4 copy-start

commit v2 on v1

--- a/solution.py
+++ b/solution.py
@@ -111,6 +111,7 @@
     ln_out,
     lens_pair,
     dyb_all,
+    ln_own,
     ln_all,
     wcol,
     xown,
@@ -145,14 +146,16 @@
     head = pair // 2
     halfrows = count // 2
     dyb[...] = cot[...].astype(BF)
-    ln_all[me.n] = lnb[...]
+    low = lnb[...].astype(BF).astype(F32)
+    ln_own[...] = low
+    ln_all[me.n] = low
     lens_pair[me.k] = lens[...]
     greet_all(dp, seq)
 
     def send_ln(j, carry):
         other = lax.rem(me.n + j, me.total)
         remote(
-            lnb, ln_all.at[me.n], ln_sem.at[0], ln_sem.at[1], (other // seq, lax.rem(other, seq))
+            ln_own, ln_all.at[me.n], ln_sem.at[0], ln_sem.at[1], (other // seq, lax.rem(other, seq))
         ).start()
         return carry
 
@@ -964,7 +967,7 @@
     rank = lax.axis_index("dp") * seq + lax.axis_index("seq")
     fit = LANES // share
     lane = jnp.arange(LANES)
-    gains = jnp.tile(ln_params.astype(BF).astype(F32), (1, fit))
+    gains = jnp.tile(ln_params, (1, fit))
     lnb = jnp.where((lane // share == rank % fit)[None, :], gains, 0.0)
     lnb = jnp.pad(lnb, ((0, 4), (0, 0)))
     lens = jnp.pad(lengths, ((0, 7), (0, LANES - lengths.shape[1])))
@@ -986,6 +989,7 @@
             shape((group, count, width), BF),
         ),
         [
+            vm((8, LANES), F32),
             vm((ranks, 8, LANES), F32),
             vm((3, wr * seq, 2 * block), BF),
             vm((count, width), BF),

time: 401 us -> 401 us (level)
  no operation moved by 1% of the time
where the time goes in v2:
time: 401 us
  Pallas kernels  384 us (96%)
  local copies, waits for them, and re-layouts  9.93 us (2%)
  other arithmetic  5.65 us (1%)
    pallas_call x4, Pallas kernels, call(): pl.pallas_call(kernel, out_shape=tuple(outs), in_specs=[vmem] * len(opera...  384 us

profile of v2, /device:TPU:0, one launch (start us, length us, event | category | flops | bytes accessed | tf_op | source)
XLA Modules:
  0.0 400.6 jit_solution(16622956918770143956)
XLA Ops:
  0.7 1.3 pad.9.lens
  1.9 0.7 tile.4
  2.6 0.1 tile.10
  2.7 0.6 pad.8.lnb
  3.3 1.5 convert_element_type.12.wo
  4.8 1.7 convert_bitcast_fusion.1.wq
  6.5 2.4 convert_bitcast_fusion.wf
  8.9 81.7 %gather.1 = (bf16[1024,1024]{1,0:T(8,128)(2,1)}, bf16[3,1024,256]{2,1,0:T(8,128)(2,1)}, bf16[1024,1024]{1,0:T(8,128)(2,1)}, f32[8,1024]{1,0:T(8,128)}, s32[2,8,1...) custom-call(f32[256,1024]{1,0:T(8,128)} %bitcast.13, f32[8,128]{1,0:T(8,128)} %pad.8.lnb, s32[8,128]{1,0:T(8,128)} %pad.9.lens, ...), custom_call_target="tpu_custom_call" | custom-call | flops 1000000 | bytes 16777216 | tf_op jit(solution)/shard_map/gather/pallas_call | solution.py:936
  90.7 76.3 %attend.1 = (bf16[1024,256]{1,0:T(8,128)(2,1)}, bf16[1024,256]{1,0:T(8,128)(2,1)}, bf16[1024,256]{1,0:T(8,128)(2,1)}, f32[1024,128]{1,0:T(8,128)}, f32[1024,128]...) custom-call(bf16[1024,1024]{1,0:T(8,128)(2,1)} %get-tuple-element.33, ...), custom_call_target="tpu_custom_call" | custom-call | flops 4000000000 | bytes 16777216 | tf_op jit(solution)/shard_map/attend/pallas_call | solution.py:936
  167.0 83.8 %ffn.1 = (f32[256,1024]{1,0:T(8,128)}, f32[256,1024]{1,0:T(8,128)}, f32[8,1024]{1,0:T(8,128)}, bf16[4,256,1024]{2,1,0:T(8,128)(2,1)}, bf16[3,512,1024]{2,1,0:T(8,128)(2,1)}) custom-call(f32[256,1024]{1,0:T(8,128)} %bitcast.14, bf16[4,256,256]{2,1,0:T(8,128)(2,1)} %get-tuple-element.36.mixed_in, bf16[1024,1024]{1,0:T(8,128)(2,1)} %get-tuple-element.37.wo, ...), custom_call_target="tpu_custom_call" | custom-call | flops 20000000000 | bytes 16777216 | tf_op jit(solution)/shard_map/ffn/pallas_call | solution.py:936
  250.8 142.6 %back.1 = (f32[256,1024]{1,0:T(8,128)}, f32[256,1024]{1,0:T(8,128)}, f32[8,128]{1,0:T(8,128)}, f32[3,32,1024]{2,1,0:T(8,128)}, f32[32,1024]{1,0:T(8,128)}, /*index=5*/f32[3,128,1024]{2,1,0:T(8,128)}) custom-call(f32[256,1024]{1,0:T(8,128)} %bitcast.15, f32[256,1024]{1,0:T(8,128)} %get-tuple-element.41.mid, f32[256,1024]{1,0:T(8,128)} %get-tuple-element.42.dmid, ...), custom_call_target="tpu_custom_call" | custom-call | flops 8000000000 | bytes 16777216 | tf_op jit(solution)/shard_map/back/pallas_call | solution.py:936
  393.3 0.0 copy-start.1
  393.3 1.4 constant_dynamic-slice_fusion
  394.7 0.0 copy-start.2
  394.8 0.0 copy-start.3
  394.8 2.4 copy.18
  397.1 0.0 copy-done.1
  397.1 0.0 copy-start
  397.1 1.0 copy.19
  398.1 0.0 copy-done.2
  398.1 0.7 copy.20
  398.8 0.0 copy-done.3
  398.8 0.7 copy.21
  399.5 0.0 copy-done
  399.5 1.1 copy.22
  (2 shorter events, 0.0 us)
Async XLA Ops:
  393.3 3.8 copy-start.1
  394.7 3.3 copy-start.2
  394.8 4.1 %copy-start.3 = (f32[32,1024]{1,0:T(8,128)S(1)}, f32[32,1024]{1,0:T(8,128)}, u32[]{:S(2)}) copy-start(f32[32,1024]{1,0:T(8,128)} %get-tuple-element.70) | copy-start | bytes 393220
  397.1 2.4 copy-start

commit v3 on v0

v3 whole, which is shorter than its diff:
```python
import functools
import math
import types

import jax
import jax.numpy as jnp
from jax import lax
from jax.experimental import pallas as pl
from jax.experimental.pallas import tpu as pltpu
from jax.sharding import PartitionSpec as P

HEAD_DIM = 64
GROUP = 8
LANES = 128
BF = jnp.bfloat16
F32 = jnp.float32
MESH = pl.DeviceIdType.MESH
NT = (((1,), (1,)), ((), ()))
NN = (((1,), (0,)), ((), ()))
TN = (((0,), (0,)), ((), ()))
EPS = 1e-05
VMEM_BYTES = 62 * 2**20


def dot(a, b, dims):
    return lax.dot_general(a, b, dims, preferred_element_type=F32)


def remote(src, dst, send, recv, device):
    return pltpu.make_async_remote_copy(
        src_ref=src, dst_ref=dst, send_sem=send, recv_sem=recv, device_id=device, device_id_type=MESH
    )


def local(src, dst, sem):
    return pltpu.make_async_copy(src, dst, sem)


class Place:
    def __init__(self, dp, seq):
        self.dp, self.seq = dp, seq
        self.d, self.s = lax.axis_index("dp"), lax.axis_index("seq")
        self.c, self.k = self.d // 2, lax.rem(self.d, 2)
        self.sib = self.d + 1 - 2 * self.k
        self.chips = dp // 2
        self.group = min(dp, GROUP)
        self.groups = dp // self.group
        self.g, self.p = self.d // self.group, lax.rem(self.d, self.group)
        self.gc = self.p // 2
        self.gchips = self.group // 2
        self.half = seq // 2
        self.r, self.h = self.s // self.half, lax.rem(self.s, self.half)
        self.hg = 2 * self.h + self.k
        self.n = self.d * seq + self.s
        self.total = dp * seq

    def of_rank(self, rank):
        return (rank // self.seq, lax.rem(rank, self.seq))

    def in_group(self, chip, core):
        return self.g * self.group + 2 * chip + core


def normalise(value):
    mean = jnp.mean(value, axis=-1, keepdims=True)
    centred = value - mean
    var = jnp.mean(centred * centred, axis=-1, keepdims=True)
    scale = lax.rsqrt(var + EPS)
    return centred * scale, scale


def norm_back(grad, normal, scale, gain):
    scaled = grad * gain
    return scale * (
        scaled
        - jnp.mean(scaled, axis=-1, keepdims=True)
        - normal * jnp.mean(scaled * normal, axis=-1, keepdims=True)
    )


def swap_halves(value):
    half = HEAD_DIM // 2
    width = value.shape[1]
    lane = lax.broadcasted_iota(jnp.int32, value.shape, 1)
    up = pltpu.roll(value, width - half, 1)
    down = pltpu.roll(value, half, 1)
    return jnp.where(lax.rem(lane, HEAD_DIM) < half, up, down)


def head_mask(shape, h):
    lane = lax.broadcasted_iota(jnp.int32, shape, 1)
    return jnp.logical_and(lane >= h * HEAD_DIM, lane < (h + 1) * HEAD_DIM)


def tall(value, rows):
    return pl.multiple_of(value, rows)


def meet(me):
    barrier = pltpu.get_barrier_semaphore()

    def hello(j, carry):
        other = lax.rem(me.n + j, me.total)
        pl.semaphore_signal(barrier, inc=1, device_id=me.of_rank(other), device_id_type=MESH)
        return carry

    lax.fori_loop(1, me.total, hello, 0)


def met(me):
    pl.semaphore_wait(pltpu.get_barrier_semaphore(), me.total - 1)


def send_or_keep(here, src, dst, send, recv, device):
    @pl.when(jnp.logical_not(here))
    def _():
        remote(src, dst, send, recv, device).start()

    @pl.when(here)
    def _():
        local(src, dst, recv).start()


def sent(here, src, send, device):
    @pl.when(jnp.logical_not(here))
    def _():
        remote(src, src, send, send, device).wait_send()


def arrived(dst, recv):
    local(dst, dst, recv).wait()


def layer_kernel(names, dp, seq, segs, *refs):
    b = types.SimpleNamespace(**dict(zip(names, refs)))
    me = Place(dp, seq)
    count, width = b.out.shape
    total = count * seq
    wr = b.og.shape[0]
    cr = wr * seq
    block = b.q.shape[1]
    heads = block // HEAD_DIM
    units = b.fg.shape[1]
    held = b.wf_full.shape[1]
    band = me.groups * units
    nc = me.gchips
    sib = (me.sib, me.s)
    share = b.ln.shape[1]
    fit = LANES // share
    tiles = width // LANES
    per = me.total // tiles
    halfrows = count // 2
    last = []

    meet(me)
    loads = [
        local(b.tok, b.out, b.load.at[0]),
        local(b.wq, b.qg, b.load.at[1]),
        local(b.wo, b.og, b.load.at[2]),
        local(b.wf, b.fg, b.load.at[3]),
        local(b.cot, b.ig, b.load.at[4]),
    ]
    for copy in loads:
        copy.start()
    b.lens_own[...] = jnp.zeros_like(b.lens_own)
    b.lens_own[0:1, 0:segs] = b.lens[...]
    b.lens_pair[me.k] = b.lens_own[...]
    gains = jnp.concatenate([b.ln[...].astype(BF).astype(F32)] * fit, axis=1)
    lane = lax.broadcasted_iota(jnp.int32, gains.shape, 1)
    b.ln_own[...] = jnp.zeros_like(b.ln_own)
    b.ln_own[0:4, :] = jnp.where(lane // share == lax.rem(me.n, fit), gains, 0.0)
    b.ln_all[me.n] = b.ln_own[...]
    loads[1].wait()
    b.wq_own[...] = b.qg[...].astype(BF)
    loads[0].wait()
    normal, _ = normalise(b.out[...])
    b.norm[...] = normal
    met(me)

    def send_ln(j, carry):
        other = lax.rem(me.n + j, me.total)
        remote(
            b.ln_own, b.ln_all.at[me.n], b.lns.at[0], b.lns.at[1], me.of_rank(other)
        ).start()
        return carry

    lax.fori_loop(1, me.total, send_ln, 0)
    len_copy = remote(b.lens_own, b.lens_pair.at[me.k], b.lens_sem.at[0], b.lens_sem.at[1], sib)
    len_copy.start()
    pair = 2 * block
    row0 = tall(me.s * wr, wr)
    out0 = tall(me.n * wr, wr)
    wq_first = []
    for j in range(1, seq):
        to = lax.rem(me.s + j, seq)
        col = tall(lax.rem(to, me.half) * pair, pair)
        wq_first.append(
            remote(
                b.wq_own.at[:, :, pl.ds(col, pair)],
                b.wcol.at[:, pl.ds(row0, wr), :],
                b.wq1s.at[j],
                b.wq1r.at[j],
                (me.d, to),
            )
        )
    for copy in wq_first:
        copy.start()
    own_wq = local(
        b.wq_own.at[:, :, pl.ds(tall(me.h * pair, pair), pair)],
        b.wcol.at[:, pl.ds(row0, wr), :],
        b.load.at[5],
    )
    own_wq.start()
    loads[2].wait()
    b.wo_full[pl.ds(out0, wr), :] = b.og[...].astype(BF)
    rest = b.ln_all.at[pl.ds(0, me.total - 1)]
    remote(rest, rest, b.lns.at[0], b.lns.at[1], sib).wait()
    for t in range(tiles):
        part = b.ln_all[t * per]
        for i in range(1, per):
            part = part + b.ln_all[t * per + i]
        b.gain[:, t * LANES : (t + 1) * LANES] = part
    b.xown[...] = (b.norm[...] * b.gain[0:1, :] + b.gain[1:2, :]).astype(BF)
    rows0 = tall(me.s * count, count)
    for j in range(me.half):
        to = me.k * me.half + lax.rem(me.h + j, me.half)
        for core in range(2):
            src = b.xown.at[pl.ds(core * halfrows, halfrows), :]
            dst = b.xrow.at[pl.ds(rows0 + core * halfrows, halfrows), :]
            here = jnp.logical_and(to == me.s, core == me.k)
            send_or_keep(
                here, src, dst, b.xs.at[j, core], b.xr.at[me.s], (2 * me.c + core, to)
            )
            last.append(
                functools.partial(sent, here, src, b.xs.at[j, core], (2 * me.c + core, to))
            )
    wo_own = b.wo_full.at[pl.ds(out0, wr), :]
    wo_first = []
    for j in range(1, seq):
        to = (me.d, lax.rem(me.s + j, seq))
        wo_first.append(remote(wo_own, wo_own, b.wo1s.at[j], b.wo1r.at[j], to))
    for copy in wo_first:
        copy.start()
    for copy in wq_first:
        copy.wait()
    own_wq.wait()
    crow0 = tall(me.d * cr, cr)

    def send_wq(j, carry):
        to = lax.rem(me.d + j, dp)
        remote(
            b.wcol.at[:, :, pl.ds(tall(lax.rem(to, 2) * block, block), block)],
            b.wq_full.at[:, pl.ds(crow0, cr), :],
            b.wq2s.at[j],
            b.wq2r.at[j],
            (to, me.s),
        ).start()
        return carry

    lax.fori_loop(1, dp, send_wq, 0)
    own_half = local(
        b.wcol.at[:, :, pl.ds(tall(me.k * block, block), block)],
        b.wq_full.at[:, pl.ds(crow0, cr), :],
        b.load.at[6],
    )
    own_half.start()
    len_copy.wait()
    row = b.lens_pair[me.r]
    place_row = lax.broadcasted_iota(jnp.int32, (8, total), 1)
    place_col = lax.broadcasted_iota(jnp.int32, (total, LANES), 0)
    end = jnp.zeros((1, 1), jnp.int32)
    segr = jnp.zeros((8, total), jnp.int32)
    segc = jnp.zeros((total, LANES), jnp.int32)
    begin = jnp.zeros((total, LANES), jnp.int32)
    for j in range(segs):
        length = row[0:1, j : j + 1]
        end = end + length
        segr = segr + (place_row >= end).astype(jnp.int32)
        past = place_col >= end
        segc = segc + past.astype(jnp.int32)
        begin = begin + jnp.where(past, length, 0)
    b.seg_row[...] = segr
    b.seg_col[...] = segc
    half = HEAD_DIM // 2
    lane = lax.broadcasted_iota(jnp.int32, (1, LANES), 1)
    rate = jnp.exp(lax.rem(lane, half).astype(F32) * (-math.log(10000.0) / half))
    angle = (place_col - begin).astype(F32) * rate
    b.cos[...] = jnp.cos(angle)
    b.sin[...] = jnp.sin(angle) * jnp.where(lax.rem(lane, HEAD_DIM) < half, -1.0, 1.0)
    loads[4].wait()
    b.dyb[me.p] = b.ig[...].astype(BF)
    loads[3].wait()
    own_units = pl.ds(tall(me.s * band + me.g * units, units), units)
    b.wf_full[:, own_units, :] = b.fg[...].astype(BF)
    for j in range(seq):
        source = lax.rem(me.s + j, seq)
        part = b.xrow.at[pl.ds(tall(source * count + me.k * halfrows, halfrows), halfrows), :]
        arrived(part, b.xr.at[source])
        remote(part, part, b.xfs.at[j], b.xfr.at[j], sib).start()
    for j in range(1, me.groups):
        other = lax.rem(me.g + j, me.groups)
        mine = b.wf_full.at[:, own_units, :]
        remote(
            mine, mine, b.fgs.at[j], b.fgr_sem.at[j], (other * me.group + me.p, me.s)
        ).start()
    for j in range(1, me.groups):
        mine = b.wf_full.at[:, own_units, :]
        remote(mine, mine, b.fgs.at[j], b.fgr_sem.at[j], sib).wait()

    def column(at):
        return b.wf_full.at[:, pl.ds(tall(at * band, band), band), :]

    def hop(t):
        for way, step in ((0, 1), (1, -1)):
            at, to = me.s - step * t, me.s + step

            @pl.when((at >= 0) & (at < seq) & (to >= 0) & (to < seq))
            def _(way=way, at=at, to=to):
                remote(
                    column(at), column(at), b.hs.at[way, t], b.hr.at[way, t], (me.d, to)
                ).start()

    def hop_in(t):
        for way, step in ((0, 1), (1, -1)):
            at = me.s - step * (t + 1)

            @pl.when((at >= 0) & (at < seq))
            def _(way=way, at=at):
                arrived(column(at), b.hr.at[way, t])

    def hop_out(t):
        for way, step in ((0, 1), (1, -1)):
            at, to = me.s - step * t, me.s + step

            @pl.when((at >= 0) & (at < seq) & (to >= 0) & (to < seq))
            def _(way=way, at=at, to=to):
                remote(
                    column(at), column(at), b.hs.at[way, t], b.hr.at[way, t], (me.d, to)
                ).wait_send()

    hop(0)
    for j in range(seq):
        part = b.xrow.at[pl.ds(0, halfrows), :]
        arrived(part, b.xfr.at[j])
        last.append(functools.partial(sent, False, part, b.xfs.at[j], sib))

    def wait_wq(j, carry):
        part = b.wq_full.at[:, pl.ds(0, cr), :]
        remote(part, part, b.wq2s.at[j], b.wq2r.at[j], sib).wait()
        return carry

    lax.fori_loop(1, dp, wait_wq, 0)
    own_half.wait()
    for copy in wo_first:
        copy.wait()
    mine = b.wo_full.at[pl.ds(crow0, cr), :]
    remote(mine, mine, b.wo3s.at[0], b.wo3r.at[0], sib).start()
    for j in range(1, me.chips):
        to = 2 * lax.rem(me.c + j, me.chips) + me.k
        remote(mine, mine, b.wo2s.at[j], b.wo2r.at[j], (to, me.s)).start()
    dy_own = b.dyb.at[me.p]
    remote(dy_own, dy_own, b.dyfs.at[0], b.dyfr.at[0], sib).start()
    for j in range(1, nc):
        to = me.in_group(lax.rem(me.gc + j, nc), me.k)
        remote(dy_own, dy_own, b.dys.at[j], b.dyr.at[j], (to, me.s)).start()

    def project(i, carry):
        rows = pl.ds(tall(i * count, count), count)
        x = b.xrow[rows, :]
        cosine = jnp.concatenate([b.cos[rows, :]] * (block // LANES), axis=1)
        sine = jnp.concatenate([b.sin[rows, :]] * (block // LANES), axis=1)
        raw = dot(x, b.wq_full[0], NN)
        b.q[rows, :] = (raw * cosine + swap_halves(raw) * sine).astype(BF)
        raw = dot(x, b.wq_full[1], NN)
        b.kk[rows, :] = (raw * cosine + swap_halves(raw) * sine).astype(BF)
        b.v[rows, :] = dot(x, b.wq_full[2], NN).astype(BF)
        return carry

    lax.fori_loop(0, seq, project, 0)
    owner = 2 * me.c + me.r

    def attend(step, carry):
        i = lax.rem(me.s + step, seq)
        rows = pl.ds(tall(i * count, count), count)
        q = b.q[rows, :]
        bias = jnp.where(b.seg_col[rows, 0:1] == b.seg_row[0:1, :], 0.0, -1e30)
        lane = lax.broadcasted_iota(jnp.int32, (count, LANES), 1)
        lse = jnp.zeros((count, LANES), F32)
        out = jnp.zeros((count, block), F32)
        for h in range(heads):
            mask = head_mask((count, block), h)
            score = dot(jnp.where(mask, q, jnp.zeros_like(q)), b.kk[...], NT) * 0.125 + bias
            top = jnp.max(score, axis=1, keepdims=True)
            weight = jnp.exp(score - top)
            tally = jnp.sum(weight, axis=1, keepdims=True)
            prob = (weight * (1.0 / tally)).astype(BF)
            out = jnp.where(mask, dot(prob, b.v[...], NN), out)
            lse = jnp.where(lane == h, top + jnp.log(tally), lse)
        b.lse[rows, :] = lse
        b.mixed[i] = out.astype(BF)
        here = jnp.logical_and(i == me.s, owner == me.d)
        send_or_keep(
            here, b.mixed.at[i], b.mixed_in.at[me.hg], b.ms.at[i], b.mr.at[me.hg], (owner, i)
        )

        @pl.when(step == 1)
        def _():
            hop_in(0)
            hop(1)

        return carry

    lax.fori_loop(0, seq, attend, 0)
    for j in range(1, me.chips):
        source = 2 * lax.rem(me.c + me.chips - j, me.chips) + me.k
        part = b.wo_full.at[pl.ds(tall(source * cr, cr), cr), :]
        arrived(part, b.wo2r.at[j])
        remote(part, part, b.wo3s.at[j], b.wo3r.at[j], sib).start()
        last.append(functools.partial(sent, False, part, b.wo2s.at[j], sib))
        last.append(functools.partial(sent, False, part, b.wo3s.at[j], sib))
    last.append(functools.partial(sent, False, mine, b.wo3s.at[0], sib))
    for j in range(me.chips):
        arrived(mine, b.wo3r.at[j])
    for j in range(seq):
        arrived(b.mixed_in.at[j], b.mr.at[j])
    mid = b.out[...]
    for h in range(seq):
        mid = mid + dot(b.mixed_in[h], b.wo_full[h * block : (h + 1) * block, :], NN)
    b.out[...] = mid
    normal, scale = normalise(mid)
    b.norm[...] = normal
    b.scale[...] = jnp.broadcast_to(scale, b.scale.shape)
    b.xall[me.gc, me.k] = (normal * b.gain[2:3, :] + b.gain[3:4, :]).astype(BF)
    x_own = b.xall.at[me.gc, me.k]
    remote(x_own, x_own, b.xfs2.at[0], b.xfr2.at[0], sib).start()
    for j in range(1, nc):
        to = me.in_group(lax.rem(me.gc + j, nc), me.k)
        remote(x_own, x_own, b.xs2.at[j], b.xr2.at[j], (to, me.s)).start()
    for j in range(1, nc):
        source = 2 * lax.rem(me.gc + nc - j, nc) + me.k
        part = b.dyb.at[source]
        arrived(part, b.dyr.at[j])
        remote(part, part, b.dyfs.at[j], b.dyfr.at[j], sib).start()
        last.append(functools.partial(sent, False, part, b.dys.at[j], sib))
        last.append(functools.partial(sent, False, part, b.dyfs.at[j], sib))
    last.append(functools.partial(sent, False, dy_own, b.dyfs.at[0], sib))
    for j in range(nc):
        arrived(dy_own, b.dyfr.at[j])
    for t in range(1, seq - 1):
        hop_in(t)
        if t + 1 < seq - 1:
            hop(t + 1)
    tile = min(256, held)
    cols = 256

    def chip(j, carry):
        cj = lax.rem(me.gc + nc - j, nc)

        @pl.when(j > 0)
        def _():
            part = b.xall.at[cj, me.k]
            arrived(part, b.xr2.at[j])
            remote(part, part, b.xfs2.at[j], b.xfr2.at[j], sib).start()

        arrived(b.xall.at[cj, 1 - me.k], b.xfr2.at[j])
        rows = pl.ds(tall(cj * 2 * count, 2 * count), 2 * count)
        x = b.xall[cj].reshape(2 * count, width)
        dy = b.dyb[pl.ds(2 * cj, 2)].reshape(2 * count, width)
        for t in range(held // tile):
            span = slice(t * tile, (t + 1) * tile)
            gate = dot(x, b.wf_full[0, span, :], NT)
            up = dot(x, b.wf_full[1, span, :], NT)
            dh = dot(dy, b.wf_full[2, span, :], NT)
            sigma = 1.0 / (1.0 + jnp.exp(-gate))
            active = gate * sigma
            b.act[2, rows, span] = (active * up).astype(BF)
            b.act[0, rows, span] = (dh * up * (sigma * (1.0 + gate * (1.0 - sigma)))).astype(BF)
            b.act[1, rows, span] = (dh * active).astype(BF)
        for t in range(width // cols):
            span = slice(t * cols, (t + 1) * cols)
            value = dot(b.act[0, rows, :], b.wf_full[0, :, span], NN)
            value = value + dot(b.act[1, rows, :], b.wf_full[1, :, span], NN)
            b.dpart[lax.rem(j, 2), :, :, span] = value.astype(BF).reshape(2, count, cols)
        part = b.dpart.at[lax.rem(j, 2), 1 - me.k]
        remote(part, b.dsib.at[j], b.dss.at[j], b.dsr.at[j], sib).start()
        remote(b.dsib.at[j], b.dsib.at[j], b.dss.at[j], b.dsr.at[j], sib).wait()
        value = b.dpart[lax.rem(j, 2), me.k].astype(F32) + b.dsib[j].astype(F32)
        b.dsum[j] = value.astype(BF)

        @pl.when(j > 0)
        def _():
            to = (me.in_group(cj, me.k), me.s)
            remote(b.dsum.at[j], b.drecv.at[j - 1], b.dps.at[j], b.dpr.at[j], to).start()

        return carry

    lax.fori_loop(0, nc, chip, 0)
    for j in range(nc):
        last.append(functools.partial(sent, False, x_own, b.xfs2.at[j], sib))
        if j:
            last.append(functools.partial(sent, False, x_own, b.xs2.at[j], sib))
    for copy in last:
        copy()
    last.clear()
    for t in range(seq - 1):
        hop_out(t)

    def add_branch(j):
        arrived(b.dsib.at[j], b.bsr.at[j])
        value = b.dpart[lax.rem(j, 2), me.k].astype(F32) + b.dsib[j].astype(F32)
        value = value.astype(BF)

        @pl.when(j == 0)
        def _():
            b.xown[...] = value

        @pl.when(j > 0)
        def _():
            remote(b.dsum.at[j], b.drecv.at[j - 1], b.dps.at[j], b.dpr.at[j], sib).wait_send()
            b.dsum[j] = value
            cj = lax.rem(me.gc + nc - j, nc)
            to = (me.in_group(cj, me.k), me.s)
            remote(b.dsum.at[j], b.brr.at[j - 1], b.brs.at[j], b.brr_sem.at[j], to).start()

    def branch(j, carry):
        cj = lax.rem(me.gc + nc - j, nc)
        rows = pl.ds(tall(cj * 2 * count, 2 * count), 2 * count)

        @pl.when(j > 1)
        def _():
            sent(False, b.dpart.at[0, 0], b.bss.at[j - 2], sib)

        for t in range(width // cols):
            span = slice(t * cols, (t + 1) * cols)
            value = dot(b.act[2, rows, :], b.wf_full[2, :, span], NN)
            b.dpart[lax.rem(j, 2), :, :, span] = value.astype(BF).reshape(2, count, cols)

        @pl.when(j > 0)
        def _():
            add_branch(j - 1)

        part = b.dpart.at[lax.rem(j, 2), 1 - me.k]
        remote(part, b.dsib.at[j], b.bss.at[j], b.bsr.at[j], sib).start()
        return carry

    lax.fori_loop(0, nc, branch, 0)

    def grads(t, carry):
        span = pl.ds(tall(t * tile, tile), tile)
        x = b.xall[...].reshape(nc * 2 * count, width)
        dy = b.dyb[...].reshape(nc * 2 * count, width)
        b.wf_full[0, span, :] = dot(b.act[0, :, span], x, TN).astype(BF)
        b.wf_full[1, span, :] = dot(b.act[1, :, span], x, TN).astype(BF)
        b.wf_full[2, span, :] = dot(b.act[2, :, span], dy, TN).astype(BF)
        return carry

    lax.fori_loop(0, held // tile, grads, 0)
    add_branch(nc - 1)
    for j in range(max(nc - 2, 0), nc):
        sent(False, b.dpart.at[0, 0], b.bss.at[j], sib)
    dn2 = b.dsum[0].astype(F32)
    for j in range(1, nc):
        arrived(b.drecv.at[j - 1], b.dpr.at[j])
        dn2 = dn2 + b.drecv[j - 1].astype(F32)
    normal = b.norm[...]
    gain2 = jnp.sum(dn2 * normal, axis=0, keepdims=True)
    shift2 = jnp.sum(dn2, axis=0, keepdims=True)
    b.lnp[...] = jnp.zeros_like(b.lnp)
    for t in range(tiles):
        lanes = slice(t * LANES, (t + 1) * LANES)
        b.lnp[t, 2:3, :] = gain2[:, lanes]
        b.lnp[t, 3:4, :] = shift2[:, lanes]
    dmid = b.ig[...] + norm_back(dn2, normal, b.scale[:, 0:1], b.gain[2:3, :])
    b.ig[...] = dmid
    dmb = dmid.astype(BF)
    for i in range(seq):
        here = jnp.logical_and(i == me.s, owner == me.d)
        sent(here, b.mixed.at[i], b.ms.at[i], sib)
    for hg in range(seq):
        b.mixed[hg] = dot(dmb, b.wo_full[hg * block : (hg + 1) * block, :], NT).astype(BF)
        to = (2 * me.c + hg % 2, me.k * me.half + hg // 2)
        here = jnp.logical_and(to[0] == me.d, to[1] == me.s)
        send_or_keep(
            here, b.mixed.at[hg], b.dmix_row.at[me.s], b.dms.at[hg], b.dmr.at[me.s], to
        )
        last.append(functools.partial(sent, here, b.mixed.at[hg], b.dms.at[hg], sib))
    slots = me.groups * seq
    slot = me.s * me.groups + me.g
    for j in range(1, slots):
        other = lax.rem(slot + j, slots)
        to = (lax.rem(other, me.groups) * me.group + me.p, other // me.groups)
        src = b.wf_full.at[:, pl.ds(tall(other * units, units), units), :]
        remote(src, b.fgr.at[j - 1], b.gs.at[j], b.gr.at[j], to).start()
    pieces = width // 2 // count

    def og_rows(parity):
        return b.dyb.at[pl.ds(parity * pieces, pieces)]

    for h in range(seq):
        part = dot(b.mixed_in[h], dmb, TN).astype(BF)
        for t in range(block // cr):
            first = h * (block // cr) + t
            row = (first // 2) * cr
            b.dyb[(first % 2) * pieces + row // count, row % count : row % count + cr, :] = part[
                t * cr : (t + 1) * cr
            ]
    remote(og_rows(1 - me.k), b.ogsib, b.o1.at[0], b.o1.at[1], sib).start()
    for j in range(seq):
        arrived(b.dmix_row.at[j], b.dmr.at[j])
    b.dk[...] = jnp.zeros_like(b.dk)
    b.dv[...] = jnp.zeros_like(b.dv)

    def og_sum():
        remote(b.ogsib, b.ogsib, b.o1.at[0], b.o1.at[1], sib).wait()
        for i in range(pieces):
            value = b.dyb[me.k * pieces + i].astype(F32) + b.ogsib[i].astype(F32)
            b.dyb[2 * pieces + i] = value.astype(BF)

        def send_og(j, carry):
            chip = lax.rem(me.c + j, me.chips)
            row = chip * cr
            src = b.dyb.at[2 * pieces + row // count, pl.ds(tall(lax.rem(row, count), cr), cr), :]
            remote(src, b.ogpl.at[j], b.o2s.at[j], b.o2r.at[j], (2 * chip + me.k, me.s)).start()
            return carry

        lax.fori_loop(1, me.chips, send_og, 0)

    def og_column():
        row = me.c * cr
        at = pl.ds(tall(lax.rem(row, count), cr), cr)
        acc = b.dyb[2 * pieces + row // count, at, :].astype(F32)
        for j in range(1, me.chips):
            remote(b.ogpl.at[j], b.ogpl.at[j], b.o2s.at[j], b.o2r.at[j], sib).wait()
            acc = acc + b.ogpl[j].astype(F32)
        b.ogc[...] = acc.astype(BF)
        for j in range(1, seq):
            to = lax.rem(me.s + j, seq)
            src = b.ogc.at[pl.ds(tall(to * wr, wr), wr), :]
            remote(src, b.ogz.at[j], b.o3s.at[j], b.o3r.at[j], (me.d, to)).start()

    def attend_back(i, carry):
        rows = pl.ds(tall(i * count, count), count)
        q = b.q[rows, :]
        dm = b.dmix_row[i]
        lse = b.lse[rows, :]
        bias = jnp.where(b.seg_col[rows, 0:1] == b.seg_row[0:1, :], 0.0, -1e30)
        grad_q = jnp.zeros((count, block), F32)
        for h in range(heads):
            mask = head_mask((count, block), h)
            qh = jnp.where(mask, q, jnp.zeros_like(q))
            dmh = jnp.where(mask, dm, jnp.zeros_like(dm))
            score = dot(qh, b.kk[...], NT) * 0.125 + bias
            prob = jnp.exp(score - lse[:, h : h + 1])
            dprob = dot(dmh, b.v[...], NT)
            centre = jnp.sum(prob * dprob, axis=1, keepdims=True)
            ds = (0.125 * prob * (dprob - centre)).astype(BF)
            grad_q = jnp.where(mask, dot(ds, b.kk[...], NN), grad_q)
            b.dk[...] += dot(ds, qh, TN)
            b.dv[...] += dot(prob.astype(BF), dmh, TN)
        cosine = jnp.concatenate([b.cos[rows, :]] * (block // LANES), axis=1)
        sine = jnp.concatenate([b.sin[rows, :]] * (block // LANES), axis=1)
        b.act[0, rows, 0:block] = (grad_q * cosine - swap_halves(grad_q) * sine).astype(BF)

        @pl.when(i == 0)
        def _():
            og_sum()

        return carry

    lax.fori_loop(0, seq, attend_back, 0)

    def back_chunk(i):
        rows = pl.ds(tall(i * count, count), count)
        cosine = jnp.concatenate([b.cos[rows, :]] * (block // LANES), axis=1)
        sine = jnp.concatenate([b.sin[rows, :]] * (block // LANES), axis=1)
        grad_k = b.dk[rows, :]
        dk = (grad_k * cosine - swap_halves(grad_k) * sine).astype(BF)
        dv = b.dv[rows, :].astype(BF)
        b.act[1, rows, 0:block] = dk
        b.act[2, rows, 0:block] = dv
        value = dot(b.act[0, rows, 0:block], b.wq_full[0], NT)
        value = value + dot(dk, b.wq_full[1], NT) + dot(dv, b.wq_full[2], NT)
        at = lax.rem(i, 2) * me.half + i // 2
        b.xall[at // 2, lax.rem(at, 2)] = value.astype(BF)

    def other_half(j, carry):
        back_chunk(2 * j + 1 - me.k)
        return carry

    def own_half_chunks(j, carry):
        back_chunk(2 * j + me.k)
        return carry

    lax.fori_loop(0, me.half, other_half, 0)
    quarter = me.half // 2
    dn_other = b.xall.at[pl.ds((1 - me.k) * quarter, quarter)]
    remote(dn_other, b.dnsib, b.n1.at[0], b.n1.at[1], sib).start()
    lax.fori_loop(0, me.half, own_half_chunks, 0)
    remote(b.dnsib, b.dnsib, b.n1.at[0], b.n1.at[1], sib).wait()
    for j in range(me.half):
        value = b.xall[me.k * quarter + j // 2, j % 2].astype(F32)
        b.dpart[0, j] = (value + b.dnsib[j // 2, j % 2].astype(F32)).astype(BF)
        i = 2 * j + me.k
        here = jnp.logical_and(owner == me.d, i == me.s)
        send_or_keep(
            here, b.dpart.at[0, j], b.dnr.at[me.h], b.n2s.at[j], b.n2r.at[me.h], (owner, i)
        )
        last.append(functools.partial(sent, here, b.dpart.at[0, j], b.n2s.at[j], sib))
    span_rows = 2 * cr
    per_tile = block // span_rows

    def qkv_terms(j, carry):
        at = lax.rem(me.c // per_tile + j, width // block)
        x = b.xrow[:, pl.ds(tall(at * block, block), block)]
        rows = pl.ds(tall(total + at * block, block), block)
        for t in range(3):
            b.act[t, rows, 0:block] = dot(x, b.act[t, 0:total, 0:block], TN).astype(BF)
        for i in range(per_tile):
            chip = at * per_tile + i

            @pl.when(chip != me.c)
            def _(chip=chip):
                src = b.act.at[:, pl.ds(tall(total + chip * span_rows, span_rows), span_rows), 0:block]
                to = (2 * chip + me.k, me.s)
                remote(src, b.qgpl.at[me.c], b.q1s.at[chip], b.q1r.at[me.c], to).start()

        return carry

    lax.fori_loop(1, width // block, qkv_terms, 0)
    qkv_terms(0, 0)
    og_column()
    tok = local(b.tok, b.norm, b.load.at[0])
    tok.start()
    dn1 = jnp.zeros((count, width), F32)
    tok.wait()
    normal, scale = normalise(b.norm[...])
    for h in range(me.half):
        arrived(b.dnr.at[h], b.n2r.at[h])
        dn1 = dn1 + b.dnr[h].astype(F32)
    b.ig[...] = b.ig[...] + norm_back(dn1, normal, scale, b.gain[0:1, :])
    gain1 = jnp.sum(dn1 * normal, axis=0, keepdims=True)
    shift1 = jnp.sum(dn1, axis=0, keepdims=True)
    for t in range(tiles):
        lanes = slice(t * LANES, (t + 1) * LANES)
        b.lnp[t, 0:1, :] = gain1[:, lanes]
        b.lnp[t, 1:2, :] = shift1[:, lanes]

    def send_lnp(j, carry):
        other = lax.rem(me.n + j, me.total)
        remote(
            b.lnp.at[other // per], b.lnr.at[me.n], b.lnt.at[0], b.lnt.at[1], me.of_rank(other)
        ).start()
        return carry

    lax.fori_loop(1, me.total, send_lnp, 0)
    b.lnr[me.n] = b.lnp[me.n // per]
    own = pl.ds(tall(total + me.c * span_rows, span_rows), span_rows)
    sums = [b.act[t, own, 0:block].astype(F32) for t in range(3)]
    for j in range(1, me.chips):
        chip = lax.rem(me.c + j, me.chips)
        part = b.qgpl.at[chip]
        remote(part, part, b.q1s.at[chip], b.q1r.at[chip], sib).wait()
        for t in range(3):
            sums[t] = sums[t] + b.qgpl[chip, t].astype(F32)
    for t in range(3):
        b.qgc[t] = sums[t].astype(BF)
    source = me.k * seq + me.s
    for core in range(2):
        for j in range(seq):
            to = lax.rem(me.s + j, seq)
            src = b.qgc.at[:, pl.ds(tall((core * seq + to) * wr, wr), wr), :]
            here = jnp.logical_and(core == me.k, to == me.s)
            send_or_keep(
                here, src, b.qgz.at[source], b.q2s.at[core, j], b.q2r.at[source], (2 * me.c + core, to)
            )
            last.append(functools.partial(sent, here, src, b.q2s.at[core, j], sib))
    value = b.out[...] + b.xown[...].astype(F32)
    for j in range(1, nc):
        remote(b.brr.at[j - 1], b.brr.at[j - 1], b.brs.at[j], b.brr_sem.at[j], sib).wait()
        value = value + b.brr[j - 1].astype(F32)
    b.out[...] = value
    acc = b.ogc[pl.ds(tall(me.s * wr, wr), wr), :].astype(F32)
    for j in range(1, seq):
        remote(b.ogz.at[j], b.ogz.at[j], b.o3s.at[j], b.o3r.at[j], sib).wait()
        acc = acc + b.ogz[j].astype(F32)
    b.og[...] = acc
    acc = b.wf_full[:, pl.ds(tall(slot * units, units), units), :].astype(F32)
    for j in range(1, slots):
        part = b.fgr.at[j - 1]
        remote(part, part, b.gs.at[j], b.gr.at[j], sib).wait()
        acc = acc + b.fgr[j - 1].astype(F32)
    b.fg[...] = acc
    rest = b.lnr.at[pl.ds(0, me.total - 1)]
    remote(rest, rest, b.lnt.at[0], b.lnt.at[1], sib).wait()
    acc = b.lnr[0]
    for j in range(1, me.total):
        acc = acc + b.lnr[j]
    b.lng[...] = acc
    for j in range(2 * seq):
        arrived(b.qgz.at[j], b.q2r.at[j])
    for hg in range(seq):
        core, h = hg % 2, hg // 2
        acc = b.qgz[core * seq + h].astype(F32) + b.qgz[core * seq + me.half + h].astype(F32)
        b.qg[:, :, hg * block : (hg + 1) * block] = acc
    for copy in last:
        copy()


def body(dp, seq, tokens, ln_params, qkv_weight, out_weight, ffn_weight, lengths, cotangent):
    count, width = tokens.shape[1], tokens.shape[2]
    ranks = dp * seq
    total = count * seq
    wr = qkv_weight.shape[0]
    cr = wr * seq
    units = ffn_weight.shape[0]
    block = width // seq
    half = seq // 2
    group = min(dp, GROUP)
    groups = dp // group
    gchips, chips, slots = group // 2, dp // 2, groups * seq
    held = units * slots
    share = ln_params.shape[1]
    sem = pltpu.SemaphoreType.DMA
    vm = pltpu.VMEM
    anywhere = pl.BlockSpec(memory_space=pl.ANY)
    vmem = pl.BlockSpec(memory_space=pltpu.VMEM)
    operands = dict(
        tok=(tokens.reshape(count, width), anywhere),
        ln=(ln_params, vmem),
        wq=(qkv_weight.transpose(1, 0, 2), anywhere),
        wo=(out_weight, anywhere),
        wf=(ffn_weight.transpose(1, 0, 2), anywhere),
        lens=(lengths, vmem),
        cot=(cotangent.reshape(count, width), anywhere),
    )
    outs = dict(
        out=(count, width),
        ig=(count, width),
        lng=(8, LANES),
        qg=(3, wr, width),
        og=(wr, width),
        fg=(3, units, width),
    )
    scratch = dict(
        norm=vm((count, width), F32),
        scale=vm((count, LANES), F32),
        lens_own=vm((8, LANES), jnp.int32),
        lens_pair=vm((2, 8, LANES), jnp.int32),
        ln_own=vm((8, LANES), F32),
        ln_all=vm((ranks, 8, LANES), F32),
        gain=vm((8, width), F32),
        wq_own=vm((3, wr, width), BF),
        wcol=vm((3, cr, 2 * block), BF),
        xown=vm((count, width), BF),
        xrow=vm((total, width), BF),
        wq_full=vm((3, width, block), BF),
        wo_full=vm((width, width), BF),
        dyb=vm((group, count, width), BF),
        q=vm((total, block), BF),
        kk=vm((total, block), BF),
        v=vm((total, block), BF),
        lse=vm((total, LANES), F32),
        cos=vm((total, LANES), F32),
        sin=vm((total, LANES), F32),
        seg_col=vm((total, LANES), jnp.int32),
        seg_row=vm((8, total), jnp.int32),
        mixed=vm((seq, count, block), BF),
        mixed_in=vm((seq, count, block), BF),
        dmix_row=vm((seq, count, block), BF),
        wf_full=vm((3, held, width), BF),
        xall=vm((gchips, 2, count, width), BF),
        act=vm((3, group * count, held), BF),
        dpart=vm((2, 2, count, width), BF),
        dsib=vm((gchips, count, width), BF),
        dsum=vm((gchips, count, width), BF),
        drecv=vm((gchips - 1, count, width), BF),
        brr=vm((gchips - 1, count, width), BF),
        ogsib=vm((width // 2 // count, count, width), BF),
        ogpl=vm((chips, cr, width), BF),
        ogc=vm((cr, width), BF),
        ogz=vm((seq, wr, width), BF),
        dk=vm((total, block), F32),
        dv=vm((total, block), F32),
        dnsib=vm((half // 2, 2, count, width), BF),
        dnr=vm((half, count, width), BF),
        qgpl=vm((chips, 3, 2 * cr, block), BF),
        qgc=vm((3, 2 * cr, block), BF),
        qgz=vm((2 * seq, 3, wr, block), BF),
        fgr=vm((slots - 1, 3, units, width), BF),
        lnp=vm((width // LANES, 8, LANES), F32),
        lnr=vm((ranks, 8, LANES), F32),
        load=sem((7,)),
        lns=sem((2,)),
        lens_sem=sem((2,)),
        wq1s=sem((seq,)),
        wq1r=sem((seq,)),
        wq2s=sem((dp,)),
        wq2r=sem((dp,)),
        wo1s=sem((seq,)),
        wo1r=sem((seq,)),
        wo2s=sem((chips,)),
        wo2r=sem((chips,)),
        wo3s=sem((chips,)),
        wo3r=sem((chips,)),
        xs=sem((half, 2)),
        xr=sem((seq,)),
        xfs=sem((seq,)),
        xfr=sem((seq,)),
        dys=sem((gchips,)),
        dyr=sem((gchips,)),
        dyfs=sem((gchips,)),
        dyfr=sem((gchips,)),
        fgs=sem((groups,)),
        fgr_sem=sem((groups,)),
        hs=sem((2, seq)),
        hr=sem((2, seq)),
        ms=sem((seq,)),
        mr=sem((seq,)),
        xs2=sem((gchips,)),
        xr2=sem((gchips,)),
        xfs2=sem((gchips,)),
        xfr2=sem((gchips,)),
        dss=sem((gchips,)),
        dsr=sem((gchips,)),
        dps=sem((gchips,)),
        dpr=sem((gchips,)),
        bss=sem((gchips,)),
        bsr=sem((gchips,)),
        brs=sem((gchips,)),
        brr_sem=sem((gchips,)),
        dms=sem((seq,)),
        dmr=sem((seq,)),
        gs=sem((slots,)),
        gr=sem((slots,)),
        o1=sem((2,)),
        o2s=sem((chips,)),
        o2r=sem((chips,)),
        o3s=sem((seq,)),
        o3r=sem((seq,)),
        n1=sem((2,)),
        n2s=sem((half,)),
        n2r=sem((half,)),
        q1s=sem((chips,)),
        q1r=sem((chips,)),
        q2s=sem((2, seq)),
        q2r=sem((2 * seq,)),
        lnt=sem((2,)),
    )
    names = (*operands, *outs, *scratch)
    out, input_grad, lng, qg, og, fg = pl.pallas_call(
        functools.partial(layer_kernel, names, dp, seq, lengths.shape[1]),
        out_shape=tuple(jax.ShapeDtypeStruct(dims, F32) for dims in outs.values()),
        in_specs=[spec for _, spec in operands.values()],
        out_specs=tuple([vmem] * len(outs)),
        scratch_shapes=list(scratch.values()),
        compiler_params=pltpu.CompilerParams(
            collective_id=1, has_side_effects=True, vmem_limit_bytes=VMEM_BYTES
        ),
        cost_estimate=pl.CostEstimate(
            flops=32 * 10**9, bytes_accessed=2**24, transcendentals=10**7
        ),
        name="layer",
    )(*[value for value, _ in operands.values()])
    rank = lax.axis_index("dp") * seq + lax.axis_index("seq")
    ln_grad = lax.dynamic_slice(lng, (0, (rank % (LANES // share)) * share), (4, share))
    return (
        out.reshape(1, count, width),
        input_grad.reshape(1, count, width),
        ln_grad,
        qg.transpose(1, 0, 2),
        og,
        fg.transpose(1, 0, 2),
    )


def solution(mesh):
    dp, seq = mesh.shape["dp"], mesh.shape["seq"]
    both = ("dp", "seq")
    in_specs = (
        P("dp", "seq", None),
        P(None, both),
        P(both, None, None),
        P(both, None),
        P(both, None, None),
        P("dp", None),
        P("dp", "seq", None),
    )
    out_specs = (
        P("dp", "seq", None),
        P("dp", "seq", None),
        P(None, both),
        P(both, None, None),
        P(both, None),
        P(both, None, None),
    )
    return jax.shard_map(
        functools.partial(body, dp, seq),
        mesh=mesh,
        in_specs=in_specs,
        out_specs=out_specs,
        check_vma=False,
    )
```

time: 2290 us -> 278 us (0.12)
  waiting for transfers between devices: 1840 us -> 0 us
  Pallas kernels: 0 us -> 269 us
  matrix products: 265 us -> 0 us
  blocking collectives: 70.3 us -> 0 us
  other arithmetic: 60 us -> 0 us
  local copies, waits for them, and re-layouts: 32 us -> 7.48 us
    reduce_scatter x5 -> x0, waiting for transfers between devices: 1550 us -> none  [the longest x1 1060 us: body(): lax.psum_scatter(make_terms(kept_hidden, kept_gate, kept_up, normed2_low,...]
    pallas_call x0 -> x1, Pallas kernels: none -> 269 us  [body(): pl.pallas_call(functools.partial(layer_kernel, names, dp, seq, lengths.sh...]
    dot_general x127 -> x0, matrix products: 265 us -> none  [the longest x32 47 us: head_scores(): jnp.einsum('qd,kd->qk', q_head, k_head, preferred_element_type=jnp.float32)]
    all_gather x5 -> x0, waiting for transfers between devices: 236 us -> none  [the longest x1 154 us: body(): lax.all_gather(ffn_low, ('dp', 'seq'), axis=0, tiled=True)]
    all_gather x1 -> x0, blocking collectives: 70.3 us -> none  [body(): lax.all_gather(masters[0], ('dp', 'seq'), axis=1, tiled=True)]
    unnamed x12 -> x0, waiting for transfers between devices: 52.9 us -> none
    another operation x9 -> x0, other arithmetic: 36.8 us -> none  [the longest x1 34 us: make_terms(): return jnp.stack([gate_term, up_term, down_term], axis=1)]
  transfers between devices with their start and end apart: 11 -> 0, of which waited for: 10 -> 0; matrix products, arithmetic and copies ran while one was open for 7% -> 0% of each run, Pallas kernels for 0% -> 0%
where the time goes in v3:
time: 278 us; the launch traced here: 277 us
  Pallas kernels  269 us (97%)
  local copies, waits for them, and re-layouts  7.48 us (3%)
    pallas_call x1, Pallas kernels, body(): pl.pallas_call(functools.partial(layer_kernel, names, dp, seq, lengths.sh...  269 us
    unnamed x13, local copies, waits for them, and re-layouts  6.06 us

profile of v3, /device:TPU:0, one launch (start us, length us, event | category | flops | bytes accessed | tf_op | source)
XLA Modules:
  0.0 277.3 jit_solution(9629699735717735894)
XLA Ops:
  0.7 269.1 %layer.1 = (f32[256,1024]{1,0:T(8,128)}, f32[256,1024]{1,0:T(8,128)}, f32[8,128]{1,0:T(8,128)}, f32[3,32,1024]{2,1,0:T(8,128)}, f32[32,1024]{1,0:T(8,128)}, /*index=5*/f32[3,128,1024]{2,1,0:T(8,128)}) custom-call(f32[256,1024]{1,0:T(8,128)} %bitcast.13, f32[4,32]{1,0:T(4,128)} %refs_1_.1, f32[3,32,1024]{2,1,0:T(8,128)} %bitcast.15, f32[32,1024]{1,0:T(8,128)} %refs_3_.1, ...), custom_call_target="tpu_custom_call" | custom-call | flops 32000000000 | bytes 16777216 | tf_op jit(solution)/shard_map/layer/pallas_call | solution.py:950
  269.8 0.0 copy-start.1
  269.8 1.4 constant_dynamic-slice_fusion
  271.2 2.3 copy.18
  273.5 0.0 copy-done.1
  273.5 0.0 copy-start.2
  273.5 0.0 copy-start.3
  273.5 0.0 copy-start
  273.5 1.0 copy.19
  274.5 0.2 copy-done.2
  274.7 0.7 copy.20
  275.5 0.0 copy-done.3
  275.5 0.7 copy.21
  276.1 0.0 copy-done
  276.1 1.1 copy.22
Async XLA Ops:
  269.8 3.7 %copy-start.1 = (f32[256,1024]{1,0:T(8,128)S(1)}, f32[256,1024]{1,0:T(8,128)}, u32[]{:S(2)}) copy-start(f32[256,1024]{1,0:T(8,128)} %get-tuple-element.13) | copy-start | bytes 3145732
  273.5 1.2 copy-start.2
  273.5 2.0 copy-start.3
  273.5 2.6 copy-start

commit v4 on v3

--- a/solution.py
+++ b/solution.py
@@ -151,6 +151,22 @@
     per = me.total // tiles
     halfrows = count // 2
     last = []
+
+    def by_rows(step):
+        def one(i, carry):
+            step(pl.ds(tall(i * some, some), some))
+            return carry
+
+        lax.fori_loop(0, count // some, one, 0)
+
+    some = 64
+    results = ("out", "ig", "lng", "qg", "og", "fg")
+    stores = []
+
+    def store(i):
+        name = results[i]
+        stores.append(local(getattr(b, name), getattr(b, name + "_out"), b.keep.at[i]))
+        stores[-1].start()
 
     meet(me)
     loads = [
@@ -173,8 +189,11 @@
     loads[1].wait()
     b.wq_own[...] = b.qg[...].astype(BF)
     loads[0].wait()
-    normal, _ = normalise(b.out[...])
-    b.norm[...] = normal
+
+    def first_norm(rows):
+        b.norm[rows, :] = normalise(b.out[rows, :])[0]
+
+    by_rows(first_norm)
     met(me)
 
     def send_ln(j, carry):
@@ -220,7 +239,11 @@
         for i in range(1, per):
             part = part + b.ln_all[t * per + i]
         b.gain[:, t * LANES : (t + 1) * LANES] = part
-    b.xown[...] = (b.norm[...] * b.gain[0:1, :] + b.gain[1:2, :]).astype(BF)
+
+    def first_out(rows):
+        b.xown[rows, :] = (b.norm[rows, :] * b.gain[0:1, :] + b.gain[1:2, :]).astype(BF)
+
+    by_rows(first_out)
     rows0 = tall(me.s * count, count)
     for j in range(me.half):
         to = me.k * me.half + lax.rem(me.h + j, me.half)
@@ -234,13 +257,6 @@
             last.append(
                 functools.partial(sent, here, src, b.xs.at[j, core], (2 * me.c + core, to))
             )
-    wo_own = b.wo_full.at[pl.ds(out0, wr), :]
-    wo_first = []
-    for j in range(1, seq):
-        to = (me.d, lax.rem(me.s + j, seq))
-        wo_first.append(remote(wo_own, wo_own, b.wo1s.at[j], b.wo1r.at[j], to))
-    for copy in wo_first:
-        copy.start()
     for copy in wq_first:
         copy.wait()
     own_wq.wait()
@@ -267,26 +283,34 @@
     len_copy.wait()
     row = b.lens_pair[me.r]
     place_row = lax.broadcasted_iota(jnp.int32, (8, total), 1)
-    place_col = lax.broadcasted_iota(jnp.int32, (total, LANES), 0)
-    end = jnp.zeros((1, 1), jnp.int32)
+    ends = [row[0:1, 0:1]]
+    for j in range(1, segs):
+        ends.append(ends[-1] + row[0:1, j : j + 1])
     segr = jnp.zeros((8, total), jnp.int32)
-    segc = jnp.zeros((total, LANES), jnp.int32)
-    begin = jnp.zeros((total, LANES), jnp.int32)
-    for j in range(segs):
-        length = row[0:1, j : j + 1]
-        end = end + length
+    for end in ends:
         segr = segr + (place_row >= end).astype(jnp.int32)
-        past = place_col >= end
-        segc = segc + past.astype(jnp.int32)
-        begin = begin + jnp.where(past, length, 0)
-    b.seg_row[...] = segr
-    b.seg_col[...] = segc
+    b.seg_row[...] = segr.astype(F32)
     half = HEAD_DIM // 2
     lane = lax.broadcasted_iota(jnp.int32, (1, LANES), 1)
     rate = jnp.exp(lax.rem(lane, half).astype(F32) * (-math.log(10000.0) / half))
-    angle = (place_col - begin).astype(F32) * rate
-    b.cos[...] = jnp.cos(angle)
-    b.sin[...] = jnp.sin(angle) * jnp.where(lax.rem(lane, HEAD_DIM) < half, -1.0, 1.0)
+    sign = jnp.where(lax.rem(lane, HEAD_DIM) < half, -1.0, 1.0)
+
+    def angles(i, carry):
+        rows = pl.ds(tall(i * LANES, LANES), LANES)
+        place = lax.broadcasted_iota(jnp.int32, (LANES, LANES), 0) + i * LANES
+        segment = jnp.zeros((LANES, LANES), jnp.int32)
+        begin = jnp.zeros((LANES, LANES), jnp.int32)
+        for end in ends:
+            past = place >= end
+            segment = segment + past.astype(jnp.int32)
+            begin = jnp.where(past, end, begin)
+        b.lse[rows, :] = segment.astype(F32)
+        angle = (place - begin).astype(F32) * rate
+        b.cos[rows, :] = jnp.cos(angle)
+        b.sin[rows, :] = jnp.sin(angle) * sign
+        return carry
+
+    lax.fori_loop(0, total // LANES, angles, 0)
     loads[4].wait()
     b.dyb[me.p] = b.ig[...].astype(BF)
     loads[3].wait()
@@ -297,6 +321,13 @@
         part = b.xrow.at[pl.ds(tall(source * count + me.k * halfrows, halfrows), halfrows), :]
         arrived(part, b.xr.at[source])
         remote(part, part, b.xfs.at[j], b.xfr.at[j], sib).start()
+    wo_own = b.wo_full.at[pl.ds(out0, wr), :]
+    wo_first = []
+    for j in range(1, seq):
+        to = (me.d, lax.rem(me.s + j, seq))
+        wo_first.append(remote(wo_own, wo_own, b.wo1s.at[j], b.wo1r.at[j], to))
+    for copy in wo_first:
+        copy.start()
     for j in range(1, me.groups):
         other = lax.rem(me.g + j, me.groups)
         mine = b.wf_full.at[:, own_units, :]
@@ -307,38 +338,26 @@
         mine = b.wf_full.at[:, own_units, :]
         remote(mine, mine, b.fgs.at[j], b.fgr_sem.at[j], sib).wait()
 
-    def column(at):
-        return b.wf_full.at[:, pl.ds(tall(at * band, band), band), :]
-
-    def hop(t):
-        for way, step in ((0, 1), (1, -1)):
-            at, to = me.s - step * t, me.s + step
-
-            @pl.when((at >= 0) & (at < seq) & (to >= 0) & (to < seq))
-            def _(way=way, at=at, to=to):
-                remote(
-                    column(at), column(at), b.hs.at[way, t], b.hr.at[way, t], (me.d, to)
-                ).start()
-
-    def hop_in(t):
-        for way, step in ((0, 1), (1, -1)):
-            at = me.s - step * (t + 1)
-
-            @pl.when((at >= 0) & (at < seq))
-            def _(way=way, at=at):
-                arrived(column(at), b.hr.at[way, t])
-
-    def hop_out(t):
-        for way, step in ((0, 1), (1, -1)):
-            at, to = me.s - step * t, me.s + step
-
-            @pl.when((at >= 0) & (at < seq) & (to >= 0) & (to < seq))
-            def _(way=way, at=at, to=to):
-                remote(
-                    column(at), column(at), b.hs.at[way, t], b.hr.at[way, t], (me.d, to)
-                ).wait_send()
-
-    hop(0)
+    near, far = me.s + 1 - 2 * lax.rem(me.s, 2), lax.rem(me.s + 2, seq)
+    beyond = lax.rem(near + 2, seq)
+
+    def column(m, at):
+        return b.wf_full.at[m, pl.ds(tall(at * band, band), band), :]
+
+    def unit_copy(way, m):
+        part = column(m, far if way == 2 else me.s)
+        to = (me.d, near if way else far)
+        return remote(part, part, b.hs.at[way, m], b.hr.at[way, m], to)
+
+    def send_units(m):
+        unit_copy(0, m).start()
+        unit_copy(1, m).start()
+
+    def pass_units(m):
+        arrived(column(m, far), b.hr.at[0, m])
+        unit_copy(2, m).start()
+
+    send_units(0)
     for j in range(seq):
         part = b.xrow.at[pl.ds(0, halfrows), :]
         arrived(part, b.xfr.at[j])
@@ -351,19 +370,6 @@
 
     lax.fori_loop(1, dp, wait_wq, 0)
     own_half.wait()
-    for copy in wo_first:
-        copy.wait()
-    mine = b.wo_full.at[pl.ds(crow0, cr), :]
-    remote(mine, mine, b.wo3s.at[0], b.wo3r.at[0], sib).start()
-    for j in range(1, me.chips):
-        to = 2 * lax.rem(me.c + j, me.chips) + me.k
-        remote(mine, mine, b.wo2s.at[j], b.wo2r.at[j], (to, me.s)).start()
-    dy_own = b.dyb.at[me.p]
-    remote(dy_own, dy_own, b.dyfs.at[0], b.dyfr.at[0], sib).start()
-    for j in range(1, nc):
-        to = me.in_group(lax.rem(me.gc + j, nc), me.k)
-        remote(dy_own, dy_own, b.dys.at[j], b.dyr.at[j], (to, me.s)).start()
-
     def project(i, carry):
         rows = pl.ds(tall(i * count, count), count)
         x = b.xrow[rows, :]
@@ -378,14 +384,27 @@
 
     lax.fori_loop(0, seq, project, 0)
     owner = 2 * me.c + me.r
+    mine = b.wo_full.at[pl.ds(crow0, cr), :]
+    for copy in wo_first:
+        copy.wait()
+    remote(mine, mine, b.wo3s.at[0], b.wo3r.at[0], sib).start()
+    for j in range(1, me.chips):
+        to = 2 * lax.rem(me.c + j, me.chips) + me.k
+        remote(mine, mine, b.wo2s.at[j], b.wo2r.at[j], (to, me.s)).start()
+    dy_own = b.dyb.at[me.p]
+    remote(dy_own, dy_own, b.dyfs.at[0], b.dyfr.at[0], sib).start()
+    for j in range(1, nc):
+        to = me.in_group(lax.rem(me.gc + j, nc), me.k)
+        remote(dy_own, dy_own, b.dys.at[j], b.dyr.at[j], (to, me.s)).start()
 
     def attend(step, carry):
         i = lax.rem(me.s + step, seq)
         rows = pl.ds(tall(i * count, count), count)
         q = b.q[rows, :]
-        bias = jnp.where(b.seg_col[rows, 0:1] == b.seg_row[0:1, :], 0.0, -1e30)
+        segment = b.lse[rows, LANES - 1 : LANES]
+        bias = jnp.where(segment == b.seg_row[0:1, :], 0.0, -1e30)
         lane = lax.broadcasted_iota(jnp.int32, (count, LANES), 1)
-        lse = jnp.zeros((count, LANES), F32)
+        lse = b.lse[rows, :]
         out = jnp.zeros((count, block), F32)
         for h in range(heads):
             mask = head_mask((count, block), h)
@@ -403,14 +422,11 @@
             here, b.mixed.at[i], b.mixed_in.at[me.hg], b.ms.at[i], b.mr.at[me.hg], (owner, i)
         )
 
-        @pl.when(step == 1)
-        def _():
-            hop_in(0)
-            hop(1)
-
         return carry
 
     lax.fori_loop(0, seq, attend, 0)
+    send_units(1)
+    send_units(2)
     for j in range(1, me.chips):
         source = 2 * lax.rem(me.c + me.chips - j, me.chips) + me.k
         part = b.wo_full.at[pl.ds(tall(source * cr, cr), cr), :]
@@ -423,19 +439,26 @@
         arrived(mine, b.wo3r.at[j])
     for j in range(seq):
         arrived(b.mixed_in.at[j], b.mr.at[j])
-    mid = b.out[...]
-    for h in range(seq):
-        mid = mid + dot(b.mixed_in[h], b.wo_full[h * block : (h + 1) * block, :], NN)
-    b.out[...] = mid
-    normal, scale = normalise(mid)
-    b.norm[...] = normal
-    b.scale[...] = jnp.broadcast_to(scale, b.scale.shape)
-    b.xall[me.gc, me.k] = (normal * b.gain[2:3, :] + b.gain[3:4, :]).astype(BF)
+    for t in range(width // block):
+        span = slice(t * block, (t + 1) * block)
+        part = b.out[:, span]
+        for h in range(seq):
+            part = part + dot(b.mixed_in[h], b.wo_full[h * block : (h + 1) * block, span], NN)
+        b.out[:, span] = part
+
+    def second_norm(rows):
+        normal, scale = normalise(b.out[rows, :])
+        b.norm[rows, :] = normal
+        b.scale[rows, :] = jnp.broadcast_to(scale, (some, LANES))
+        b.xall[me.gc, me.k, rows, :] = (normal * b.gain[2:3, :] + b.gain[3:4, :]).astype(BF)
+
+    by_rows(second_norm)
     x_own = b.xall.at[me.gc, me.k]
     remote(x_own, x_own, b.xfs2.at[0], b.xfr2.at[0], sib).start()
     for j in range(1, nc):
         to = me.in_group(lax.rem(me.gc + j, nc), me.k)
         remote(x_own, x_own, b.xs2.at[j], b.xr2.at[j], (to, me.s)).start()
+    pass_units(0)
     for j in range(1, nc):
         source = 2 * lax.rem(me.gc + nc - j, nc) + me.k
         part = b.dyb.at[source]
@@ -446,15 +469,30 @@
     last.append(functools.partial(sent, False, dy_own, b.dyfs.at[0], sib))
     for j in range(nc):
         arrived(dy_own, b.dyfr.at[j])
-    for t in range(1, seq - 1):
-        hop_in(t)
-        if t + 1 < seq - 1:
-            hop(t + 1)
-    tile = min(256, held)
+    tile = 2 * band
     cols = 256
-
-    def chip(j, carry):
+    near_tile = me.s // 2
+
+    def chip_rows(j):
         cj = lax.rem(me.gc + nc - j, nc)
+        return cj, pl.ds(tall(cj * 2 * count, 2 * count), 2 * count)
+
+    def hidden(j, t):
+        cj, rows = chip_rows(j)
+        span = pl.ds(tall(t * tile, tile), tile)
+        x = b.xall[cj].reshape(2 * count, width)
+        dy = b.dyb[pl.ds(2 * cj, 2)].reshape(2 * count, width)
+        gate = dot(x, b.wf_full[0, span, :], NT)
+        up = dot(x, b.wf_full[1, span, :], NT)
+        dh = dot(dy, b.wf_full[2, span, :], NT)
+        sigma = 1.0 / (1.0 + jnp.exp(-gate))
+        active = gate * sigma
+        b.act[2, rows, span] = (active * up).astype(BF)
+        b.act[0, rows, span] = (dh * up * (sigma * (1.0 + gate * (1.0 - sigma)))).astype(BF)
+        b.act[1, rows, span] = (dh * active).astype(BF)
+
+    def near_units(j, carry):
+        cj, _ = chip_rows(j)
 
         @pl.when(j > 0)
         def _():
@@ -462,20 +500,39 @@
             arrived(part, b.xr2.at[j])
             remote(part, part, b.xfs2.at[j], b.xfr2.at[j], sib).start()
 
+        @pl.when((j > 0) & (j < 3))
+        def _():
+            pass_units(j)
+
         arrived(b.xall.at[cj, 1 - me.k], b.xfr2.at[j])
-        rows = pl.ds(tall(cj * 2 * count, 2 * count), 2 * count)
-        x = b.xall[cj].reshape(2 * count, width)
-        dy = b.dyb[pl.ds(2 * cj, 2)].reshape(2 * count, width)
-        for t in range(held // tile):
-            span = slice(t * tile, (t + 1) * tile)
-            gate = dot(x, b.wf_full[0, span, :], NT)
-            up = dot(x, b.wf_full[1, span, :], NT)
-            dh = dot(dy, b.wf_full[2, span, :], NT)
-            sigma = 1.0 / (1.0 + jnp.exp(-gate))
-            active = gate * sigma
-            b.act[2, rows, span] = (active * up).astype(BF)
-            b.act[0, rows, span] = (dh * up * (sigma * (1.0 + gate * (1.0 - sigma)))).astype(BF)
-            b.act[1, rows, span] = (dh * active).astype(BF)
+        hidden(j, near_tile)
+        return carry
+
+    def far_units(j, carry):
+        hidden(j, 1 - near_tile)
+        return carry
+
+    for m in range(3):
+        arrived(column(m, near), b.hr.at[1, m])
+    lax.fori_loop(0, nc, near_units, 0)
+    for m in range(3):
+        arrived(column(m, beyond), b.hr.at[2, m])
+    lax.fori_loop(0, nc, far_units, 0)
+
+    def take_dn2(j):
+        part = b.dsib.at[j]
+        remote(part, part, b.dss.at[j], b.dsr.at[j], sib).wait()
+        value = b.dpart[lax.rem(j, 2), me.k].astype(F32) + b.dsib[j].astype(F32)
+        b.dsum[j] = value.astype(BF)
+
+        @pl.when(j > 0)
+        def _():
+            to = (me.in_group(chip_rows(j)[0], me.k), me.s)
+            remote(b.dsum.at[j], b.drecv.at[j - 1], b.dps.at[j], b.dpr.at[j], to).start()
+
+    def grad_tokens(i, carry):
+        j = nc - 1 - i
+        _, rows = chip_rows(j)
         for t in range(width // cols):
             span = slice(t * cols, (t + 1) * cols)
             value = dot(b.act[0, rows, :], b.wf_full[0, :, span], NN)
@@ -483,18 +540,15 @@
             b.dpart[lax.rem(j, 2), :, :, span] = value.astype(BF).reshape(2, count, cols)
         part = b.dpart.at[lax.rem(j, 2), 1 - me.k]
         remote(part, b.dsib.at[j], b.dss.at[j], b.dsr.at[j], sib).start()
-        remote(b.dsib.at[j], b.dsib.at[j], b.dss.at[j], b.dsr.at[j], sib).wait()
-        value = b.dpart[lax.rem(j, 2), me.k].astype(F32) + b.dsib[j].astype(F32)
-        b.dsum[j] = value.astype(BF)
-
-        @pl.when(j > 0)
+
+        @pl.when(i > 0)
         def _():
-            to = (me.in_group(cj, me.k), me.s)
-            remote(b.dsum.at[j], b.drecv.at[j - 1], b.dps.at[j], b.dpr.at[j], to).start()
-
-        return carry
-
-    lax.fori_loop(0, nc, chip, 0)
+            take_dn2(j + 1)
+
+        return carry
+
+    lax.fori_loop(0, nc, grad_tokens, 0)
+    take_dn2(0)
     for j in range(nc):
         last.append(functools.partial(sent, False, x_own, b.xfs2.at[j], sib))
         if j:
@@ -502,9 +556,40 @@
     for copy in last:
         copy()
     last.clear()
-    for t in range(seq - 1):
-        hop_out(t)
-
+    for m in range(3):
+        for way in range(3):
+            unit_copy(way, m).wait_send()
+    bg = (b.wf_full.at[0], b.wf_full.at[1], b.down)
+
+    def grads(t, then):
+        span = pl.ds(tall(t * tile, tile), tile)
+        tokens = nc * 2 * count
+        for m in range(3):
+            left = b.act[m, :, span].T
+            for c in range(width // cols):
+                part = slice(c * cols, (c + 1) * cols)
+                if m < 2:
+                    right = b.xall[:, :, :, part].reshape(tokens, cols)
+                else:
+                    right = b.dyb[:, :, part].reshape(tokens, cols)
+                bg[m][span, part] = dot(left, right, NN).astype(BF)
+            then(m)
+
+    def band_rows(at):
+        return pl.ds(tall(at * band, band), band)
+
+    def send_terms(stage, at, to, m):
+        src = bg[m].at[band_rows(at), :]
+        remote(src, b.rs.at[stage, m], b.gs.at[stage, m], b.gr.at[stage, m], (me.d, to)).start()
+
+    def cross_terms(m):
+        arrived(b.rs.at[0, m], b.gr.at[0, m])
+        value = bg[m][band_rows(far), :].astype(F32) + b.rs[0, m].astype(F32)
+        bg[m][band_rows(far), :] = value.astype(BF)
+        send_terms(2, far, far, m)
+
+    grads(1 - near_tile, lambda m: send_terms(0, beyond, near, m))
+    grads(near_tile, lambda m: None)
     def add_branch(j):
         arrived(b.dsib.at[j], b.bsr.at[j])
         value = b.dpart[lax.rem(j, 2), me.k].astype(F32) + b.dsib[j].astype(F32)
@@ -522,22 +607,22 @@
             to = (me.in_group(cj, me.k), me.s)
             remote(b.dsum.at[j], b.brr.at[j - 1], b.brs.at[j], b.brr_sem.at[j], to).start()
 
-    def branch(j, carry):
-        cj = lax.rem(me.gc + nc - j, nc)
-        rows = pl.ds(tall(cj * 2 * count, 2 * count), 2 * count)
-
-        @pl.when(j > 1)
+    def branch(i, carry):
+        j = nc - 1 - i
+        _, rows = chip_rows(j)
+
+        @pl.when(i > 1)
         def _():
-            sent(False, b.dpart.at[0, 0], b.bss.at[j - 2], sib)
+            sent(False, b.dpart.at[0, 0], b.bss.at[j + 2], sib)
 
         for t in range(width // cols):
             span = slice(t * cols, (t + 1) * cols)
             value = dot(b.act[2, rows, :], b.wf_full[2, :, span], NN)
             b.dpart[lax.rem(j, 2), :, :, span] = value.astype(BF).reshape(2, count, cols)
 
-        @pl.when(j > 0)
+        @pl.when(i > 0)
         def _():
-            add_branch(j - 1)
+            add_branch(j + 1)
 
         part = b.dpart.at[lax.rem(j, 2), 1 - me.k]
         remote(part, b.dsib.at[j], b.bss.at[j], b.bsr.at[j], sib).start()
@@ -545,34 +630,34 @@
 
     lax.fori_loop(0, nc, branch, 0)
 
-    def grads(t, carry):
-        span = pl.ds(tall(t * tile, tile), tile)
-        x = b.xall[...].reshape(nc * 2 * count, width)
-        dy = b.dyb[...].reshape(nc * 2 * count, width)
-        b.wf_full[0, span, :] = dot(b.act[0, :, span], x, TN).astype(BF)
-        b.wf_full[1, span, :] = dot(b.act[1, :, span], x, TN).astype(BF)
-        b.wf_full[2, span, :] = dot(b.act[2, :, span], dy, TN).astype(BF)
-        return carry
-
-    lax.fori_loop(0, held // tile, grads, 0)
-    add_branch(nc - 1)
-    for j in range(max(nc - 2, 0), nc):
+    add_branch(0)
+    cross_terms(0)
+    for m in range(3):
+        send_terms(1, near, near, m)
+    for j in range(min(2, nc)):
         sent(False, b.dpart.at[0, 0], b.bss.at[j], sib)
-    dn2 = b.dsum[0].astype(F32)
     for j in range(1, nc):
         arrived(b.drecv.at[j - 1], b.dpr.at[j])
-        dn2 = dn2 + b.drecv[j - 1].astype(F32)
-    normal = b.norm[...]
-    gain2 = jnp.sum(dn2 * normal, axis=0, keepdims=True)
-    shift2 = jnp.sum(dn2, axis=0, keepdims=True)
+
+    def add_ln(row, value):
+        for t in range(tiles):
+            b.lnp[t, row : row + 1, :] += value[:, t * LANES : (t + 1) * LANES]
+
     b.lnp[...] = jnp.zeros_like(b.lnp)
-    for t in range(tiles):
-        lanes = slice(t * LANES, (t + 1) * LANES)
-        b.lnp[t, 2:3, :] = gain2[:, lanes]
-        b.lnp[t, 3:4, :] = shift2[:, lanes]
-    dmid = b.ig[...] + norm_back(dn2, normal, b.scale[:, 0:1], b.gain[2:3, :])
-    b.ig[...] = dmid
-    dmb = dmid.astype(BF)
+
+    def second_back(rows):
+        grad = b.dsum[0, rows, :].astype(F32)
+        for j in range(1, nc):
+            grad = grad + b.drecv[j - 1, rows, :].astype(F32)
+        normal = b.norm[rows, :]
+        add_ln(2, jnp.sum(grad * normal, axis=0, keepdims=True))
+        add_ln(3, jnp.sum(grad, axis=0, keepdims=True))
+        dmid = b.ig[rows, :] + norm_back(grad, normal, b.scale[rows, 0:1], b.gain[2:3, :])
+        b.ig[rows, :] = dmid
+        b.dmb[rows, :] = dmid.astype(BF)
+
+    by_rows(second_back)
+    dmb = b.dmb[...]
     for i in range(seq):
         here = jnp.logical_and(i == me.s, owner == me.d)
         sent(here, b.mixed.at[i], b.ms.at[i], sib)
@@ -584,13 +669,6 @@
             here, b.mixed.at[hg], b.dmix_row.at[me.s], b.dms.at[hg], b.dmr.at[me.s], to
         )
         last.append(functools.partial(sent, here, b.mixed.at[hg], b.dms.at[hg], sib))
-    slots = me.groups * seq
-    slot = me.s * me.groups + me.g
-    for j in range(1, slots):
-        other = lax.rem(slot + j, slots)
-        to = (lax.rem(other, me.groups) * me.group + me.p, other // me.groups)
-        src = b.wf_full.at[:, pl.ds(tall(other * units, units), units), :]
-        remote(src, b.fgr.at[j - 1], b.gs.at[j], b.gr.at[j], to).start()
     pieces = width // 2 // count
 
     def og_rows(parity):
@@ -607,6 +685,8 @@
     remote(og_rows(1 - me.k), b.ogsib, b.o1.at[0], b.o1.at[1], sib).start()
     for j in range(seq):
         arrived(b.dmix_row.at[j], b.dmr.at[j])
+    for m in range(1, 3):
+        cross_terms(m)
     b.dk[...] = jnp.zeros_like(b.dk)
     b.dv[...] = jnp.zeros_like(b.dv)
 
@@ -643,7 +723,8 @@
         q = b.q[rows, :]
         dm = b.dmix_row[i]
         lse = b.lse[rows, :]
-        bias = jnp.where(b.seg_col[rows, 0:1] == b.seg_row[0:1, :], 0.0, -1e30)
+        segment = b.lse[rows, LANES - 1 : LANES]
+        bias = jnp.where(segment == b.seg_row[0:1, :], 0.0, -1e30)
         grad_q = jnp.zeros((count, block), F32)
         for h in range(heads):
             mask = head_mask((count, block), h)
@@ -731,19 +812,21 @@
     og_column()
     tok = local(b.tok, b.norm, b.load.at[0])
     tok.start()
-    dn1 = jnp.zeros((count, width), F32)
     tok.wait()
-    normal, scale = normalise(b.norm[...])
     for h in range(me.half):
         arrived(b.dnr.at[h], b.n2r.at[h])
-        dn1 = dn1 + b.dnr[h].astype(F32)
-    b.ig[...] = b.ig[...] + norm_back(dn1, normal, scale, b.gain[0:1, :])
-    gain1 = jnp.sum(dn1 * normal, axis=0, keepdims=True)
-    shift1 = jnp.sum(dn1, axis=0, keepdims=True)
-    for t in range(tiles):
-        lanes = slice(t * LANES, (t + 1) * LANES)
-        b.lnp[t, 0:1, :] = gain1[:, lanes]
-        b.lnp[t, 1:2, :] = shift1[:, lanes]
+
+    def first_back(rows):
+        grad = b.dnr[0, rows, :].astype(F32)
+        for h in range(1, me.half):
+            grad = grad + b.dnr[h, rows, :].astype(F32)
+        normal, scale = normalise(b.norm[rows, :])
+        b.ig[rows, :] += norm_back(grad, normal, scale, b.gain[0:1, :])
+        add_ln(0, jnp.sum(grad * normal, axis=0, keepdims=True))
+        add_ln(1, jnp.sum(grad, axis=0, keepdims=True))
+
+    by_rows(first_back)
+    store(1)
 
     def send_lnp(j, carry):
         other = lax.rem(me.n + j, me.total)
@@ -779,31 +862,76 @@
         remote(b.brr.at[j - 1], b.brr.at[j - 1], b.brs.at[j], b.brr_sem.at[j], sib).wait()
         value = value + b.brr[j - 1].astype(F32)
     b.out[...] = value
+    store(0)
     acc = b.ogc[pl.ds(tall(me.s * wr, wr), wr), :].astype(F32)
     for j in range(1, seq):
         remote(b.ogz.at[j], b.ogz.at[j], b.o3s.at[j], b.o3r.at[j], sib).wait()
         acc = acc + b.ogz[j].astype(F32)
     b.og[...] = acc
-    acc = b.wf_full[:, pl.ds(tall(slot * units, units), units), :].astype(F32)
-    for j in range(1, slots):
-        part = b.fgr.at[j - 1]
-        remote(part, part, b.gs.at[j], b.gr.at[j], sib).wait()
-        acc = acc + b.fgr[j - 1].astype(F32)
-    b.fg[...] = acc
+    store(4)
+    for m in range(3):
+        for j in range(1, 3):
+            arrived(b.rs.at[j, m], b.gr.at[j, m])
+        for j in range(3):
+            last.append(functools.partial(sent, False, b.rs.at[0, 0], b.gs.at[j, m], sib))
+        acc = bg[m][band_rows(me.s), :].astype(F32)
+        acc = acc + b.rs[1, m].astype(F32) + b.rs[2, m].astype(F32)
+        if me.groups == 1:
+            b.fg[m] = acc
+        else:
+            bg[m][band_rows(me.s), :] = acc.astype(BF)
+    if me.groups > 1:
+        for m in range(3):
+            for j in range(1, me.groups):
+                other = lax.rem(me.g + j, me.groups)
+                src = bg[m].at[pl.ds(tall(me.s * band + other * units, units), units), :]
+                to = (other * me.group + me.p, me.s)
+                remote(src, b.grp.at[j, m], b.grs.at[j, m], b.grr.at[j, m], to).start()
+        for m in range(3):
+            acc = bg[m][pl.ds(tall(me.s * band + me.g * units, units), units), :].astype(F32)
+            for j in range(1, me.groups):
+                part = b.grp.at[j, m]
+                remote(part, part, b.grs.at[j, m], b.grr.at[j, m], sib).wait()
+                acc = acc + b.grp[j, m].astype(F32)
+            b.fg[m] = acc
+    store(5)
     rest = b.lnr.at[pl.ds(0, me.total - 1)]
     remote(rest, rest, b.lnt.at[0], b.lnt.at[1], sib).wait()
     acc = b.lnr[0]
     for j in range(1, me.total):
         acc = acc + b.lnr[j]
-    b.lng[...] = acc
+    for i in range(fit):
+
+        @pl.when(lax.rem(me.n, fit) == i)
+        def _(i=i):
+            b.lng[...] = acc[0:4, i * share : (i + 1) * share]
+
+    store(2)
     for j in range(2 * seq):
         arrived(b.qgz.at[j], b.q2r.at[j])
     for hg in range(seq):
         core, h = hg % 2, hg // 2
         acc = b.qgz[core * seq + h].astype(F32) + b.qgz[core * seq + me.half + h].astype(F32)
         b.qg[:, :, hg * block : (hg + 1) * block] = acc
+    store(3)
     for copy in last:
         copy()
+    for copy in stores:
+        copy.wait()
+
+
+def keep_kernel(count, *refs):
+    given, kept, held = refs[:count], refs[count : 2 * count], refs[2 * count : 3 * count]
+    sems = refs[-1]
+    ins = [local(given[i], held[i], sems.at[0, i]) for i in range(count)]
+    outs = [local(held[i], kept[i], sems.at[1, i]) for i in range(count)]
+    for copy in ins:
+        copy.start()
+    for i in range(count):
+        ins[i].wait()
+        outs[i].start()
+    for copy in outs:
+        copy.wait()
 
 
 def body(dp, seq, tokens, ln_params, qkv_weight, out_weight, ffn_weight, lengths, cotangent):
@@ -836,12 +964,13 @@
     outs = dict(
         out=(count, width),
         ig=(count, width),
-        lng=(8, LANES),
+        lng=(4, share),
         qg=(3, wr, width),
         og=(wr, width),
         fg=(3, units, width),
     )
     scratch = dict(
+        **{name: vm(dims, F32) for name, dims in outs.items()},
         norm=vm((count, width), F32),
         scale=vm((count, LANES), F32),
         lens_own=vm((8, LANES), jnp.int32),
@@ -852,6 +981,7 @@
         wq_own=vm((3, wr, width), BF),
         wcol=vm((3, cr, 2 * block), BF),
         xown=vm((count, width), BF),
+        dmb=vm((count, width), BF),
         xrow=vm((total, width), BF),
         wq_full=vm((3, width, block), BF),
         wo_full=vm((width, width), BF),
@@ -862,8 +992,7 @@
         lse=vm((total, LANES), F32),
         cos=vm((total, LANES), F32),
         sin=vm((total, LANES), F32),
-        seg_col=vm((total, LANES), jnp.int32),
-        seg_row=vm((8, total), jnp.int32),
+        seg_row=vm((8, total), F32),
         mixed=vm((seq, count, block), BF),
         mixed_in=vm((seq, count, block), BF),
         dmix_row=vm((seq, count, block), BF),
@@ -886,10 +1015,13 @@
         qgpl=vm((chips, 3, 2 * cr, block), BF),
         qgc=vm((3, 2 * cr, block), BF),
         qgz=vm((2 * seq, 3, wr, block), BF),
-        fgr=vm((slots - 1, 3, units, width), BF),
+        rs=vm((3, 3, groups * units, width), BF),
+        grp=vm((groups, 3, units, width) if groups > 1 else (8, LANES), BF),
+        down=vm((held, width), BF),
         lnp=vm((width // LANES, 8, LANES), F32),
         lnr=vm((ranks, 8, LANES), F32),
         load=sem((7,)),
+        keep=sem((6,)),
         lns=sem((2,)),
         lens_sem=sem((2,)),
         wq1s=sem((seq,)),
@@ -912,8 +1044,8 @@
         dyfr=sem((gchips,)),
         fgs=sem((groups,)),
         fgr_sem=sem((groups,)),
-        hs=sem((2, seq)),
-        hr=sem((2, seq)),
+        hs=sem((3, 3)),
+        hr=sem((3, 3)),
         ms=sem((seq,)),
         mr=sem((seq,)),
         xs2=sem((gchips,)),
@@ -930,8 +1062,10 @@
         brr_sem=sem((gchips,)),
         dms=sem((seq,)),
         dmr=sem((seq,)),
-        gs=sem((slots,)),
-        gr=sem((slots,)),
+        gs=sem((3, 3)),
+        gr=sem((3, 3)),
+        grs=sem((groups, 3)),
+        grr=sem((groups, 3)),
         o1=sem((2,)),
         o2s=sem((chips,)),
         o2r=sem((chips,)),
@@ -946,12 +1080,12 @@
         q2r=sem((2 * seq,)),
         lnt=sem((2,)),
     )
-    names = (*operands, *outs, *scratch)
-    out, input_grad, lng, qg, og, fg = pl.pallas_call(
+    names = (*operands, *[name + "_out" for name in outs], *scratch)
+    results = pl.pallas_call(
         functools.partial(layer_kernel, names, dp, seq, lengths.shape[1]),
         out_shape=tuple(jax.ShapeDtypeStruct(dims, F32) for dims in outs.values()),
         in_specs=[spec for _, spec in operands.values()],
-        out_specs=tuple([vmem] * len(outs)),
+        out_specs=tuple([anywhere] * len(outs)),
         scratch_shapes=list(scratch.values()),
         compiler_params=pltpu.CompilerParams(
             collective_id=1, has_side_effects=True, vmem_limit_bytes=VMEM_BYTES
@@ -961,8 +1095,14 @@
         ),
         name="layer",
     )(*[value for value, _ in operands.values()])
-    rank = lax.axis_index("dp") * seq + lax.axis_index("seq")
-    ln_grad = lax.dynamic_slice(lng, (0, (rank % (LANES // share)) * share), (4, share))
+    out, input_grad, ln_grad, qg, og, fg = pl.pallas_call(
+        functools.partial(keep_kernel, len(outs)),
+        out_shape=tuple(jax.ShapeDtypeStruct(dims, F32) for dims in outs.values()),
+        in_specs=[anywhere] * len(outs),
+        out_specs=tuple([anywhere] * len(outs)),
+        scratch_shapes=[*[vm(dims, F32) for dims in outs.values()], sem((2, len(outs)))],
+        name="keep",
+    )(*results)
     return (
         out.reshape(1, count, width),
         input_grad.reshape(1, count, width),

time: 278 us -> 258 us (0.928)
  Pallas kernels: 269 us -> 255 us
  local copies, waits for them, and re-layouts: 7.48 us -> 0 us
    pallas_call x1, Pallas kernels: 269 us -> 251 us  [body(): pl.pallas_call(functools.partial(layer_kernel, names, dp, seq, lengths.sh...]
    unnamed x13 -> x0, local copies, waits for them, and re-layouts: 6.06 us -> none
    pallas_call x0 -> x1, Pallas kernels: none -> 3.5 us  [body(): pl.pallas_call(functools.partial(keep_kernel, len(outs)), out_shape=tuple...]
where the time goes in v4:
time: 258 us; the launch traced here: 255 us
  Pallas kernels  255 us (99%)
    pallas_call x1, Pallas kernels, body(): pl.pallas_call(functools.partial(layer_kernel, names, dp, seq, lengths.sh...  251 us

profile of v4, /device:TPU:0, one launch (start us, length us, event | category | flops | bytes accessed | tf_op | source)
XLA Modules:
  0.0 255.4 jit_solution(14081939929662313296)
XLA Ops:
  0.6 251.0 %layer.1 = (f32[256,1024]{1,0:T(8,128)}, f32[256,1024]{1,0:T(8,128)}, f32[4,32]{1,0:T(4,128)}, f32[3,32,1024]{2,1,0:T(8,128)}, f32[32,1024]{1,0:T(8,128)}, /*index=5*/f32[3,128,1024]{2,1,0:T(8,128)}) custom-call(f32[256,1024]{1,0:T(8,128)} %bitcast.10, f32[4,32]{1,0:T(4,128)} %refs_1_.1, f32[3,32,1024]{2,1,0:T(8,128)} %bitcast.14, f32[32,1024]{1,0:T(8,128)} %refs_3_.1, ...), custom_call_target="tpu_custom_call" | custom-call | flops 32000000000 | bytes 16777216 | tf_op jit(solution)/shard_map/layer/pallas_call | solution.py:1084
  251.7 3.5 %keep.1 = (f32[256,1024]{1,0:T(8,128)}, f32[256,1024]{1,0:T(8,128)}, f32[4,32]{1,0:T(4,128)}, f32[3,32,1024]{2,1,0:T(8,128)}, f32[32,1024]{1,0:T(8,128)}, /*index=5*/f32[3,128,1024]{2,1,0:T(8,128)}) custom-call(f32[256,1024]{1,0:T(8,128)} %get-tuple-element.18.refs_0_, f32[256,1024]{1,0:T(8,128)} %get-tuple-element.19.refs_1_, ...), custom_call_target="tpu_custom_call" | custom-call | tf_op jit(solution)/shard_map/keep/pallas_call | solution.py:1098

commit v5 on v4

--- a/solution.py
+++ b/solution.py
@@ -357,7 +357,6 @@
         arrived(column(m, far), b.hr.at[0, m])
         unit_copy(2, m).start()
 
-    send_units(0)
     for j in range(seq):
         part = b.xrow.at[pl.ds(0, halfrows), :]
         arrived(part, b.xfr.at[j])
@@ -425,8 +424,8 @@
         return carry
 
     lax.fori_loop(0, seq, attend, 0)
-    send_units(1)
-    send_units(2)
+    for m in range(3):
+        send_units(m)
     for j in range(1, me.chips):
         source = 2 * lax.rem(me.c + me.chips - j, me.chips) + me.k
         part = b.wo_full.at[pl.ds(tall(source * cr, cr), cr), :]

time: 258 us -> 253 us (0.981)
  Pallas kernels: 255 us -> 252 us
    pallas_call x1, Pallas kernels: 251 us -> 248 us  [body(): pl.pallas_call(functools.partial(layer_kernel, names, dp, seq, lengths.sh...]
where the time goes in v5:
time: 253 us
  Pallas kernels  252 us (100%)
    pallas_call x1, Pallas kernels, body(): pl.pallas_call(functools.partial(layer_kernel, names, dp, seq, lengths.sh...  248 us

profile of v5, /device:TPU:0, one launch (start us, length us, event | category | flops | bytes accessed | tf_op | source)
XLA Modules:
  0.0 252.7 jit_solution(3230610148249431203)
XLA Ops:
  0.6 248.4 %layer.1 = (f32[256,1024]{1,0:T(8,128)}, f32[256,1024]{1,0:T(8,128)}, f32[4,32]{1,0:T(4,128)}, f32[3,32,1024]{2,1,0:T(8,128)}, f32[32,1024]{1,0:T(8,128)}, /*index=5*/f32[3,128,1024]{2,1,0:T(8,128)}) custom-call(f32[256,1024]{1,0:T(8,128)} %bitcast.10, f32[4,32]{1,0:T(4,128)} %refs_1_.1, f32[3,32,1024]{2,1,0:T(8,128)} %bitcast.14, f32[32,1024]{1,0:T(8,128)} %refs_3_.1, ...), custom_call_target="tpu_custom_call" | custom-call | flops 32000000000 | bytes 16777216 | tf_op jit(solution)/shard_map/layer/pallas_call | solution.py:1083
  249.0 3.5 %keep.1 = (f32[256,1024]{1,0:T(8,128)}, f32[256,1024]{1,0:T(8,128)}, f32[4,32]{1,0:T(4,128)}, f32[3,32,1024]{2,1,0:T(8,128)}, f32[32,1024]{1,0:T(8,128)}, /*index=5*/f32[3,128,1024]{2,1,0:T(8,128)}) custom-call(f32[256,1024]{1,0:T(8,128)} %get-tuple-element.18.refs_0_, f32[256,1024]{1,0:T(8,128)} %get-tuple-element.19.refs_1_, ...), custom_call_target="tpu_custom_call" | custom-call | tf_op jit(solution)/shard_map/keep/pallas_call | solution.py:1097

commit v6 on v5

--- a/solution.py
+++ b/solution.py
@@ -630,9 +630,6 @@
     lax.fori_loop(0, nc, branch, 0)
 
     add_branch(0)
-    cross_terms(0)
-    for m in range(3):
-        send_terms(1, near, near, m)
     for j in range(min(2, nc)):
         sent(False, b.dpart.at[0, 0], b.bss.at[j], sib)
     for j in range(1, nc):
@@ -684,8 +681,10 @@
     remote(og_rows(1 - me.k), b.ogsib, b.o1.at[0], b.o1.at[1], sib).start()
     for j in range(seq):
         arrived(b.dmix_row.at[j], b.dmr.at[j])
-    for m in range(1, 3):
+    for m in range(3):
         cross_terms(m)
+    for m in range(3):
+        send_terms(1, near, near, m)
     b.dk[...] = jnp.zeros_like(b.dk)
     b.dv[...] = jnp.zeros_like(b.dv)
 

time: 253 us -> 244 us (0.964)
  Pallas kernels: 252 us -> 242 us
    pallas_call x1, Pallas kernels: 248 us -> 238 us  [body(): pl.pallas_call(functools.partial(layer_kernel, names, dp, seq, lengths.sh...]
where the time goes in v6:
time: 244 us; the launch traced here: 242 us
  Pallas kernels  242 us (99%)
    pallas_call x1, Pallas kernels, body(): pl.pallas_call(functools.partial(layer_kernel, names, dp, seq, lengths.sh...  238 us

profile of v6, /device:TPU:0, one launch (start us, length us, event | category | flops | bytes accessed | tf_op | source)
XLA Modules:
  0.0 242.5 jit_solution(18087589322071628843)
XLA Ops:
  0.6 238.1 %layer.1 = (f32[256,1024]{1,0:T(8,128)}, f32[256,1024]{1,0:T(8,128)}, f32[4,32]{1,0:T(4,128)}, f32[3,32,1024]{2,1,0:T(8,128)}, f32[32,1024]{1,0:T(8,128)}, /*index=5*/f32[3,128,1024]{2,1,0:T(8,128)}) custom-call(f32[256,1024]{1,0:T(8,128)} %bitcast.10, f32[4,32]{1,0:T(4,128)} %refs_1_.1, f32[3,32,1024]{2,1,0:T(8,128)} %bitcast.14, f32[32,1024]{1,0:T(8,128)} %refs_3_.1, ...), custom_call_target="tpu_custom_call" | custom-call | flops 32000000000 | bytes 16777216 | tf_op jit(solution)/shard_map/layer/pallas_call | solution.py:1082
  238.8 3.5 %keep.1 = (f32[256,1024]{1,0:T(8,128)}, f32[256,1024]{1,0:T(8,128)}, f32[4,32]{1,0:T(4,128)}, f32[3,32,1024]{2,1,0:T(8,128)}, f32[32,1024]{1,0:T(8,128)}, /*index=5*/f32[3,128,1024]{2,1,0:T(8,128)}) custom-call(f32[256,1024]{1,0:T(8,128)} %get-tuple-element.18.refs_0_, f32[256,1024]{1,0:T(8,128)} %get-tuple-element.19.refs_1_, ...), custom_call_target="tpu_custom_call" | custom-call | tf_op jit(solution)/shard_map/keep/pallas_call | solution.py:1096

commit v7 on v6

--- a/solution.py
+++ b/solution.py
@@ -589,49 +589,6 @@
 
     grads(1 - near_tile, lambda m: send_terms(0, beyond, near, m))
     grads(near_tile, lambda m: None)
-    def add_branch(j):
-        arrived(b.dsib.at[j], b.bsr.at[j])
-        value = b.dpart[lax.rem(j, 2), me.k].astype(F32) + b.dsib[j].astype(F32)
-        value = value.astype(BF)
-
-        @pl.when(j == 0)
-        def _():
-            b.xown[...] = value
-
-        @pl.when(j > 0)
-        def _():
-            remote(b.dsum.at[j], b.drecv.at[j - 1], b.dps.at[j], b.dpr.at[j], sib).wait_send()
-            b.dsum[j] = value
-            cj = lax.rem(me.gc + nc - j, nc)
-            to = (me.in_group(cj, me.k), me.s)
-            remote(b.dsum.at[j], b.brr.at[j - 1], b.brs.at[j], b.brr_sem.at[j], to).start()
-
-    def branch(i, carry):
-        j = nc - 1 - i
-        _, rows = chip_rows(j)
-
-        @pl.when(i > 1)
-        def _():
-            sent(False, b.dpart.at[0, 0], b.bss.at[j + 2], sib)
-
-        for t in range(width // cols):
-            span = slice(t * cols, (t + 1) * cols)
-            value = dot(b.act[2, rows, :], b.wf_full[2, :, span], NN)
-            b.dpart[lax.rem(j, 2), :, :, span] = value.astype(BF).reshape(2, count, cols)
-
-        @pl.when(i > 0)
-        def _():
-            add_branch(j + 1)
-
-        part = b.dpart.at[lax.rem(j, 2), 1 - me.k]
-        remote(part, b.dsib.at[j], b.bss.at[j], b.bsr.at[j], sib).start()
-        return carry
-
-    lax.fori_loop(0, nc, branch, 0)
-
-    add_branch(0)
-    for j in range(min(2, nc)):
-        sent(False, b.dpart.at[0, 0], b.bss.at[j], sib)
     for j in range(1, nc):
         arrived(b.drecv.at[j - 1], b.dpr.at[j])
 
@@ -679,6 +636,49 @@
                 t * cr : (t + 1) * cr
             ]
     remote(og_rows(1 - me.k), b.ogsib, b.o1.at[0], b.o1.at[1], sib).start()
+    def add_branch(j):
+        arrived(b.dsib.at[j], b.bsr.at[j])
+        value = b.dpart[lax.rem(j, 2), me.k].astype(F32) + b.dsib[j].astype(F32)
+        value = value.astype(BF)
+
+        @pl.when(j == 0)
+        def _():
+            b.xown[...] = value
+
+        @pl.when(j > 0)
+        def _():
+            remote(b.dsum.at[j], b.drecv.at[j - 1], b.dps.at[j], b.dpr.at[j], sib).wait_send()
+            b.dsum[j] = value
+            cj = lax.rem(me.gc + nc - j, nc)
+            to = (me.in_group(cj, me.k), me.s)
+            remote(b.dsum.at[j], b.brr.at[j - 1], b.brs.at[j], b.brr_sem.at[j], to).start()
+
+    def branch(i, carry):
+        j = nc - 1 - i
+        _, rows = chip_rows(j)
+
+        @pl.when(i > 1)
+        def _():
+            sent(False, b.dpart.at[0, 0], b.bss.at[j + 2], sib)
+
+        for t in range(width // cols):
+            span = slice(t * cols, (t + 1) * cols)
+            value = dot(b.act[2, rows, :], b.wf_full[2, :, span], NN)
+            b.dpart[lax.rem(j, 2), :, :, span] = value.astype(BF).reshape(2, count, cols)
+
+        @pl.when(i > 0)
+        def _():
+            add_branch(j + 1)
+
+        part = b.dpart.at[lax.rem(j, 2), 1 - me.k]
+        remote(part, b.dsib.at[j], b.bss.at[j], b.bsr.at[j], sib).start()
+        return carry
+
+    lax.fori_loop(0, nc, branch, 0)
+
+    add_branch(0)
+    for j in range(min(2, nc)):
+        sent(False, b.dpart.at[0, 0], b.bss.at[j], sib)
     for j in range(seq):
         arrived(b.dmix_row.at[j], b.dmr.at[j])
     for m in range(3):

time: 244 us -> 240 us (0.984)
  Pallas kernels: 242 us -> 239 us
    pallas_call x1, Pallas kernels: 238 us -> 235 us  [body(): pl.pallas_call(functools.partial(layer_kernel, names, dp, seq, lengths.sh...]
where the time goes in v7:
time: 240 us
  Pallas kernels  239 us (100%)
    pallas_call x1, Pallas kernels, body(): pl.pallas_call(functools.partial(layer_kernel, names, dp, seq, lengths.sh...  235 us

profile of v7, /device:TPU:0, one launch (start us, length us, event | category | flops | bytes accessed | tf_op | source)
XLA Modules:
  0.0 239.6 jit_solution(5667193761135163707)
XLA Ops:
  0.6 235.3 %layer.1 = (f32[256,1024]{1,0:T(8,128)}, f32[256,1024]{1,0:T(8,128)}, f32[4,32]{1,0:T(4,128)}, f32[3,32,1024]{2,1,0:T(8,128)}, f32[32,1024]{1,0:T(8,128)}, /*index=5*/f32[3,128,1024]{2,1,0:T(8,128)}) custom-call(f32[256,1024]{1,0:T(8,128)} %bitcast.10, f32[4,32]{1,0:T(4,128)} %refs_1_.1, f32[3,32,1024]{2,1,0:T(8,128)} %bitcast.14, f32[32,1024]{1,0:T(8,128)} %refs_3_.1, ...), custom_call_target="tpu_custom_call" | custom-call | flops 32000000000 | bytes 16777216 | tf_op jit(solution)/shard_map/layer/pallas_call | solution.py:1082
  236.0 3.5 %keep.1 = (f32[256,1024]{1,0:T(8,128)}, f32[256,1024]{1,0:T(8,128)}, f32[4,32]{1,0:T(4,128)}, f32[3,32,1024]{2,1,0:T(8,128)}, f32[32,1024]{1,0:T(8,128)}, /*index=5*/f32[3,128,1024]{2,1,0:T(8,128)}) custom-call(f32[256,1024]{1,0:T(8,128)} %get-tuple-element.18.refs_0_, f32[256,1024]{1,0:T(8,128)} %get-tuple-element.19.refs_1_, ...), custom_call_target="tpu_custom_call" | custom-call | tf_op jit(solution)/shard_map/keep/pallas_call | solution.py:1096

commit v8 on v7

--- a/solution.py
+++ b/solution.py
@@ -766,17 +766,14 @@
         back_chunk(2 * j + 1 - me.k)
         return carry
 
-    def own_half_chunks(j, carry):
-        back_chunk(2 * j + me.k)
-        return carry
-
     lax.fori_loop(0, me.half, other_half, 0)
     quarter = me.half // 2
     dn_other = b.xall.at[pl.ds((1 - me.k) * quarter, quarter)]
     remote(dn_other, b.dnsib, b.n1.at[0], b.n1.at[1], sib).start()
-    lax.fori_loop(0, me.half, own_half_chunks, 0)
-    remote(b.dnsib, b.dnsib, b.n1.at[0], b.n1.at[1], sib).wait()
     for j in range(me.half):
+        back_chunk(2 * j + me.k)
+        if j == 0:
+            remote(b.dnsib, b.dnsib, b.n1.at[0], b.n1.at[1], sib).wait()
         value = b.xall[me.k * quarter + j // 2, j % 2].astype(F32)
         b.dpart[0, j] = (value + b.dnsib[j // 2, j % 2].astype(F32)).astype(BF)
         i = 2 * j + me.k

time: 240 us -> 240 us (level)
  no operation moved by 1% of the time
where the time goes in v8:
time: 240 us
  Pallas kernels  239 us (100%)
    pallas_call x1, Pallas kernels, body(): pl.pallas_call(functools.partial(layer_kernel, names, dp, seq, lengths.sh...  235 us

profile of v8, /device:TPU:0, one launch (start us, length us, event | category | flops | bytes accessed | tf_op | source)
XLA Modules:
  0.0 239.6 jit_solution(3796668683387978884)
XLA Ops:
  0.6 235.3 %layer.1 = (f32[256,1024]{1,0:T(8,128)}, f32[256,1024]{1,0:T(8,128)}, f32[4,32]{1,0:T(4,128)}, f32[3,32,1024]{2,1,0:T(8,128)}, f32[32,1024]{1,0:T(8,128)}, /*index=5*/f32[3,128,1024]{2,1,0:T(8,128)}) custom-call(f32[256,1024]{1,0:T(8,128)} %bitcast.10, f32[4,32]{1,0:T(4,128)} %refs_1_.1, f32[3,32,1024]{2,1,0:T(8,128)} %bitcast.14, f32[32,1024]{1,0:T(8,128)} %refs_3_.1, ...), custom_call_target="tpu_custom_call" | custom-call | flops 32000000000 | bytes 16777216 | tf_op jit(solution)/shard_map/layer/pallas_call | solution.py:1079
  236.0 3.5 %keep.1 = (f32[256,1024]{1,0:T(8,128)}, f32[256,1024]{1,0:T(8,128)}, f32[4,32]{1,0:T(4,128)}, f32[3,32,1024]{2,1,0:T(8,128)}, f32[32,1024]{1,0:T(8,128)}, /*index=5*/f32[3,128,1024]{2,1,0:T(8,128)}) custom-call(f32[256,1024]{1,0:T(8,128)} %get-tuple-element.18.refs_0_, f32[256,1024]{1,0:T(8,128)} %get-tuple-element.19.refs_1_, ...), custom_call_target="tpu_custom_call" | custom-call | tf_op jit(solution)/shard_map/keep/pallas_call | solution.py:1093
